TPU v7x, 32 devices: a whole 2x2x4 slice. The times are simulated.
32 devices in a mesh: tok: 16 (over z, y, x), head: 2 (over core).
Axes of the slice: x: 2, y: 2, z: 4, core: 2. Of those that a mesh axis runs over, the one named last changes fastest.
Arguments:
- queries: bfloat16 [2048, 1536], P('tok', 'head'), may hold values from -32 to 32
- keys: bfloat16 [2048, 1536], P('tok', 'head'), may hold values from -32 to 32
- values: bfloat16 [2048, 1536], P('tok', 'head'), may hold values from -6 to 6
- window: int32 [16, 27], P('tok'), may hold values from -1 to 15, as said below
- out_weight: bfloat16 [1536, 3072], P('head', 'tok'), may hold values from -0.15625 to 0.15625
Outputs:
- projected: bfloat16 [2048, 3072], P('tok', 'head')
Inputs may be any that keep to these rules, and one draw needn't show every extreme that they name: `window`: row i lists distinct tiles: first i itself, then tiles whose frame, row and column each differ from those of i by at most one; -1 marks unused entries, which come last.
All inputs are finite; a program needn't handle non-finite values.
Results may differ from a plain program's by a relative error of at most 0.015.
Values may be sent and summed in bfloat16 or wider, within the bound.
A program may use at most 128 MiB of HBM per device.

v0:
```python
import jax
import jax.numpy as jnp
from jax import lax
from jax.sharding import PartitionSpec as P

HD = 128


def passed_along(value, axis, by):
    count = lax.axis_size(axis)
    pairs = [(i, i + by) for i in range(count) if 0 <= i + by < count]
    return lax.ppermute(value, axis, pairs)


def attend_tile(running, query_heads, kv_piece, is_listed):
    peak_now, total_now, summed_now = running
    tok_rows, head_count, head_size = query_heads.shape
    key_heads = kv_piece[0].reshape(tok_rows, head_count, head_size)
    value_heads = kv_piece[1].reshape(tok_rows, head_count, head_size)
    scores = jnp.einsum("qhd,khd->hqk", query_heads, key_heads, preferred_element_type=jnp.float32)
    scores = jnp.where(is_listed, scores * HD ** (-0.5), -1e30)
    new_peak = jnp.maximum(peak_now, jnp.max(scores, axis=-1))
    rescale = jnp.exp(peak_now - new_peak)
    unrounded = jnp.exp(scores - new_peak[..., None])
    total_next = total_now * rescale + jnp.sum(unrounded, axis=-1)
    weights = unrounded.astype(jnp.bfloat16)
    summed_next = summed_now * rescale[..., None] + jnp.einsum(
        "hqk,khd->hqd", weights, value_heads, preferred_element_type=jnp.float32
    )
    return (new_peak, total_next, summed_next)


def body(queries, keys, values, window, out_weight):
    tok_rows, feat_width = queries.shape
    head_count = feat_width // HD
    tile_count = lax.axis_size("tok")
    grid_w = min(8, tile_count // 4)
    grid_h = min(4, tile_count // (2 * grid_w))
    frame_size = grid_w * grid_h
    frame_count = tile_count // frame_size
    my_tile = lax.axis_index("tok")
    my_frame = my_tile // frame_size
    my_row = my_tile // grid_w % grid_h
    my_col = my_tile % grid_w
    query_heads = queries.reshape(tok_rows, head_count, HD)
    listed_tiles = window[0]
    initial = (
        jnp.full((head_count, tok_rows), -1e30, jnp.float32),
        jnp.zeros((head_count, tok_rows), jnp.float32),
        jnp.zeros((head_count, tok_rows, HD), jnp.float32),
    )
    own_pair = jnp.stack([keys, values])
    slot_blocks = []
    for step_f in (-1, 0, 1):
        for step_h in (-1, 0, 1):
            for step_w in (-1, 0, 1):
                distance = step_f * frame_size + step_h * grid_w + step_w
                if distance == 0:
                    slot_blocks.append(own_pair)
                else:
                    slot_blocks.append(passed_along(own_pair, "tok", -distance))
    near_box = jnp.stack(slot_blocks)
    slot_range = jnp.arange(27, dtype=jnp.int32)
    slot_f = slot_range // 9 - 1
    slot_h = slot_range // 3 % 3 - 1
    slot_w = slot_range % 3 - 1
    slot_distance = slot_f * frame_size + slot_h * grid_w + slot_w
    inside = (
        (my_frame + slot_f >= 0)
        & (my_frame + slot_f < frame_count)
        & (my_row + slot_h >= 0)
        & (my_row + slot_h < grid_h)
        & (my_col + slot_w >= 0)
        & (my_col + slot_w < grid_w)
    )

    def visit_band(running, slot_index):
        key_tile = my_tile + slot_distance[slot_index]
        is_listed = inside[slot_index] & jnp.any(listed_tiles == key_tile)
        kv_piece = lax.dynamic_index_in_dim(near_box, slot_index, 0, keepdims=False)
        return (attend_tile(running, query_heads, kv_piece, is_listed), None)

    running, _ = lax.scan(visit_band, initial, slot_range)
    attended = (running[2] / running[1][..., None]).transpose(1, 0, 2).reshape(tok_rows, feat_width)
    attended = attended.astype(jnp.bfloat16)
    projection = jnp.dot(
        attended,
        lax.all_gather(out_weight, "tok", axis=1, tiled=True),
        preferred_element_type=jnp.float32,
    )
    return lax.psum_scatter(
        projection.astype(jnp.bfloat16), "head", scatter_dimension=1, tiled=True
    )


def solution(mesh):
    in_specs = (
        P("tok", "head"),
        P("tok", "head"),
        P("tok", "head"),
        P("tok", None),
        P("head", "tok"),
    )
    out_specs = P("tok", "head")
    return jax.shard_map(body, mesh=mesh, in_specs=in_specs, out_specs=out_specs, check_vma=False)
```

profile of v0, /device:TPU:11, one launch (start us, length us, event | category | flops | bytes accessed | tf_op | source)
XLA Modules:
  0.0 543.6 jit_solution(2746782539563976163)
XLA Ops:
  10.8 7.0 %collective-permute-start.3 = (bf16[2,128,768]{1,2,0:T(8,128)(2,1)S(1)}, bf16[2,128,768]{1,2,0:T(8,128)(2,1)S(1)}, u32[]{:S(2)}, u32[]{:S(2)}) collective-permute-start(bf16[2,128,768]{1,2,0:T(8,128)(2,1)S(1)} %pad_maximum_fusion), channel_id=1, source_target_pairs={{0,18},{2,20},{4,22},{6,24},{8,26},{10,28},{12,30},{1,19},{3,21},{... | collective-permute-start | bytes 1179656 | tf_op jit(solution)/shard_map/ppermute | solution.py:12
  17.8 1.3 collective-permute-start.4
  21.1 1.3 collective-permute-start.5
  22.5 1.9 collective-permute-start.6
  24.5 18.0 %collective-permute-start.7 = (bf16[2,128,768]{1,2,0:T(8,128)(2,1)S(1)}, bf16[2,128,768]{1,2,0:T(8,128)(2,1)S(1)}, u32[]{:S(2)}, u32[]{:S(2)}) collective-permute-start(bf16[2,128,768]{1,2,0:T(8,128)(2,1)S(1)} %pad_maximum_fusion), channel_id=1, source_target_pairs={{0,8},{2,10},{4,12},{6,14},{8,16},{10,18},{12,20},{14,22},{16,24},... | collective-permute-start | bytes 1179656 | tf_op jit(solution)/shard_map/ppermute | solution.py:12
  42.6 38.0 %collective-permute-done.3 = bf16[2,128,768]{1,2,0:T(8,128)(2,1)S(1)} collective-permute-done((bf16[2,128,768]{1,2,0:T(8,128)(2,1)S(1)}, bf16[2,128,768]{1,2,0:T(8,128)(2,1)S(1)}, u32[]{:S(2)}, u32[]{:S(2)}) %collective-permute-start.3) | collective-permute-done | bytes 393248 | tf_op jit(solution)/shard_map/ppermute | solution.py:12
  80.6 1.9 collective-permute-start.8
  82.5 12.2 %collective-permute-done.4 = bf16[2,128,768]{1,2,0:T(8,128)(2,1)S(1)} collective-permute-done((bf16[2,128,768]{1,2,0:T(8,128)(2,1)S(1)}, bf16[2,128,768]{1,2,0:T(8,128)(2,1)S(1)}, u32[]{:S(2)}, u32[]{:S(2)}) %collective-permute-start.4) | collective-permute-done | bytes 393248 | tf_op jit(solution)/shard_map/ppermute | solution.py:12
  94.8 3.1 collective-permute-start.9
  97.9 12.1 %collective-permute-done.5 = bf16[2,128,768]{1,2,0:T(8,128)(2,1)S(1)} collective-permute-done((bf16[2,128,768]{1,2,0:T(8,128)(2,1)S(1)}, bf16[2,128,768]{1,2,0:T(8,128)(2,1)S(1)}, u32[]{:S(2)}, u32[]{:S(2)}) %collective-permute-start.5) | collective-permute-done | bytes 393248 | tf_op jit(solution)/shard_map/ppermute | solution.py:12
  110.1 2.1 collective-permute-start.10
  112.2 6.3 %collective-permute-done.6 = bf16[2,128,768]{1,2,0:T(8,128)(2,1)S(1)} collective-permute-done((bf16[2,128,768]{1,2,0:T(8,128)(2,1)S(1)}, bf16[2,128,768]{1,2,0:T(8,128)(2,1)S(1)}, u32[]{:S(2)}, u32[]{:S(2)}) %collective-permute-start.6) | collective-permute-done | bytes 393248 | tf_op jit(solution)/shard_map/ppermute | solution.py:12
  118.5 1.9 collective-permute-start.11
  120.5 11.2 %collective-permute-done.7 = bf16[2,128,768]{1,2,0:T(8,128)(2,1)S(1)} collective-permute-done((bf16[2,128,768]{1,2,0:T(8,128)(2,1)S(1)}, bf16[2,128,768]{1,2,0:T(8,128)(2,1)S(1)}, u32[]{:S(2)}, u32[]{:S(2)}) %collective-permute-start.7) | collective-permute-done | bytes 393248 | tf_op jit(solution)/shard_map/ppermute | solution.py:12
  131.7 1.9 collective-permute-start.12
  133.7 23.6 %collective-permute-done.8 = bf16[2,128,768]{1,2,0:T(8,128)(2,1)S(1)} collective-permute-done((bf16[2,128,768]{1,2,0:T(8,128)(2,1)S(1)}, bf16[2,128,768]{1,2,0:T(8,128)(2,1)S(1)}, u32[]{:S(2)}, u32[]{:S(2)}) %collective-permute-start.8) | collective-permute-done | bytes 393248 | tf_op jit(solution)/shard_map/ppermute | solution.py:12
  157.2 1.9 collective-permute-start.13
  159.4 1.3 collective-permute-start.14
  160.8 1.3 collective-permute-start.15
  162.2 1.3 collective-permute-start.16
  164.3 9.8 %collective-permute-done.13 = bf16[2,128,768]{1,2,0:T(8,128)(2,1)S(1)} collective-permute-done((bf16[2,128,768]{1,2,0:T(8,128)(2,1)S(1)}, bf16[2,128,768]{1,2,0:T(8,128)(2,1)S(1)}, u32[]{:S(2)}, u32[]{:S(2)}) %collective-permute-start.13) | collective-permute-done | bytes 393248 | tf_op jit(solution)/shard_map/ppermute | solution.py:12
  175.0 11.8 %collective-permute-done.14 = bf16[2,128,768]{1,2,0:T(8,128)(2,1)S(1)} collective-permute-done((bf16[2,128,768]{1,2,0:T(8,128)(2,1)S(1)}, bf16[2,128,768]{1,2,0:T(8,128)(2,1)S(1)}, u32[]{:S(2)}, u32[]{:S(2)}) %collective-permute-start.14) | collective-permute-done | bytes 393248 | tf_op jit(solution)/shard_map/ppermute | solution.py:12
  187.5 6.4 %collective-permute-done.15 = bf16[2,128,768]{1,2,0:T(8,128)(2,1)S(1)} collective-permute-done((bf16[2,128,768]{1,2,0:T(8,128)(2,1)S(1)}, bf16[2,128,768]{1,2,0:T(8,128)(2,1)S(1)}, u32[]{:S(2)}, u32[]{:S(2)}) %collective-permute-start.15) | collective-permute-done | bytes 393248 | tf_op jit(solution)/shard_map/ppermute | solution.py:12
  194.0 13.4 %collective-permute-done.16 = bf16[2,128,768]{1,2,0:T(8,128)(2,1)S(1)} collective-permute-done((bf16[2,128,768]{1,2,0:T(8,128)(2,1)S(1)}, bf16[2,128,768]{1,2,0:T(8,128)(2,1)S(1)}, u32[]{:S(2)}, u32[]{:S(2)}) %collective-permute-start.16) | collective-permute-done | bytes 393248 | tf_op jit(solution)/shard_map/ppermute | solution.py:12
  207.7 4.0 copy-done
  211.7 261.8 %while.15 = (s32[]{:T(128)}, f32[6,128]{1,0:T(8,128)S(1)}, f32[6,128]{1,0:T(8,128)S(1)}, f32[6,128,128]{2,1,0:T(8,128)S(1)}, s32[27]{0:T(128)S(1)}, /*index=5*/p...) while((s32[]{:T(128)}, f32[6,128]{1,0:T(8,128)S(1)}, ...), condition=%wide.region_4.5_spmd.clone, body=%wide.region_0.4_spmd.clone.sunk | while | flops 51318588 | bytes 3391854 | solution.py:83
  216.3 1.3 compare_reduce_fusion.2
  226.0 1.3 compare_reduce_fusion.2
  235.7 1.3 compare_reduce_fusion.2
  245.4 1.3 compare_reduce_fusion.2
  255.1 1.3 compare_reduce_fusion.2
  264.8 1.3 compare_reduce_fusion.2
  272.5 1.3 dynamic_slice.23
  274.5 1.3 compare_reduce_fusion.2
  284.2 1.3 compare_reduce_fusion.2
  293.9 1.3 compare_reduce_fusion.2
  301.6 1.3 dynamic_slice.23
  303.6 1.3 compare_reduce_fusion.2
  313.3 1.3 compare_reduce_fusion.2
  321.0 1.3 dynamic_slice.23
  323.0 1.3 compare_reduce_fusion.2
  332.7 1.3 compare_reduce_fusion.2
  342.4 1.3 compare_reduce_fusion.2
  350.1 1.3 dynamic_slice.23
  352.1 1.3 compare_reduce_fusion.2
  361.8 1.3 compare_reduce_fusion.2
  369.5 1.3 dynamic_slice.23
  371.5 1.3 compare_reduce_fusion.2
  381.2 1.3 compare_reduce_fusion.2
  390.8 1.3 compare_reduce_fusion.2
  398.6 1.3 dynamic_slice.23
  400.5 1.3 compare_reduce_fusion.2
  410.2 1.3 compare_reduce_fusion.2
  418.0 1.3 dynamic_slice.23
  419.9 1.3 compare_reduce_fusion.2
  429.6 1.3 compare_reduce_fusion.2
  439.3 1.3 compare_reduce_fusion.2
  447.1 1.3 dynamic_slice.23
  449.0 1.3 compare_reduce_fusion.2
  458.7 1.3 compare_reduce_fusion.2
  466.5 1.3 dynamic_slice.23
  468.4 1.3 compare_reduce_fusion.2
  473.7 4.9 convolution_convert_fusion
  478.6 58.1 %reduce-scatter.2.cloned.1.call-done = bf16[128,1536]{1,0:T(8,128)(2,1)} async-done(((bf16[128,3072]{1,0:T(8,128)(2,1)}), bf16[128,1536]{1,0:T(8,128)(2,1)}) %reduce-scatter.2.cloned.1.call-update) | async-done | bytes 393232 | tf_op jit(solution)/shard_map/reduce_scatter | solution.py:91
  (323 shorter events, 115.2 us)
Async XLA Ops:
  6.5 467.2 %all-gather.2.cloned.1.call-start = ((), (), s32[]{:S(2)}) async-start(), calls=%async_computation.1 | async-start | bytes 5013504 | tf_op jit(solution)/shard_map/all_gather | solution.py:88
  8.8 12.4 %collective-permute-start = (bf16[2,128,768]{1,2,0:T(8,128)(2,1)S(1)}, bf16[2,128,768]{1,2,0:T(8,128)(2,1)S(1)}, u32[]{:S(2)}, u32[]{:S(2)}) collective-permute-start(bf16[2,128,768]{1,2,0:T(8,128)(2,1)S(1)} %pad_maximum_fusion), channel_id=1, source_target_pairs={{0,26},{2,28},{4,30},{1,27},{3,29},{5,31}} | collective-permute-start | bytes 1179656 | tf_op jit(solution)/shard_map/ppermute | solution.py:12
  9.5 13.0 %collective-permute-start.1 = (bf16[2,128,768]{1,2,0:T(8,128)(2,1)S(1)}, bf16[2,128,768]{1,2,0:T(8,128)(2,1)S(1)}, u32[]{:S(2)}, u32[]{:S(2)}) collective-permute-start(bf16[2,128,768]{1,2,0:T(8,128)(2,1)S(1)} %pad_maximum_fusion), channel_id=1, source_target_pairs={{0,24},{2,26},{4,28},{6,30},{1,25},{3,27},{5,29},{7,31}} | collective-permute-start | bytes 1179656 | tf_op jit(solution)/shard_map/ppermute | solution.py:12
  10.2 14.3 %collective-permute-start.2 = (bf16[2,128,768]{1,2,0:T(8,128)(2,1)S(1)}, bf16[2,128,768]{1,2,0:T(8,128)(2,1)S(1)}, u32[]{:S(2)}, u32[]{:S(2)}) collective-permute-start(bf16[2,128,768]{1,2,0:T(8,128)(2,1)S(1)} %pad_maximum_fusion), channel_id=1, source_target_pairs={{0,22},{2,24},{4,26},{6,28},{8,30},{1,23},{3,25},{5,27},{7,29},{9,... | collective-permute-start | bytes 1179656 | tf_op jit(solution)/shard_map/ppermute | solution.py:12
  10.8 69.7 %collective-permute-start.3 = (bf16[2,128,768]{1,2,0:T(8,128)(2,1)S(1)}, bf16[2,128,768]{1,2,0:T(8,128)(2,1)S(1)}, u32[]{:S(2)}, u32[]{:S(2)}) collective-permute-start(bf16[2,128,768]{1,2,0:T(8,128)(2,1)S(1)} %pad_maximum_fusion), channel_id=1, source_target_pairs={{0,18},{2,20},{4,22},{6,24},{8,26},{10,28},{12,30},{1,19},{3,21},{... | collective-permute-start | bytes 1179656 | tf_op jit(solution)/shard_map/ppermute | solution.py:12
  17.8 76.9 %collective-permute-start.4 = (bf16[2,128,768]{1,2,0:T(8,128)(2,1)S(1)}, bf16[2,128,768]{1,2,0:T(8,128)(2,1)S(1)}, u32[]{:S(2)}, u32[]{:S(2)}) collective-permute-start(bf16[2,128,768]{1,2,0:T(8,128)(2,1)S(1)} %pad_maximum_fusion), channel_id=1, source_target_pairs={{0,16},{2,18},{4,20},{6,22},{8,24},{10,26},{12,28},{14,30},{1,17},... | collective-permute-start | bytes 1179656 | tf_op jit(solution)/shard_map/ppermute | solution.py:12
  19.2 517.5 %reduce-scatter.2.cloned.1.call-start = ((), (), s32[]{:S(2)}) async-start(), calls=%async_computation.2 | async-start | bytes 1179648 | tf_op jit(solution)/shard_map/reduce_scatter | solution.py:91
  21.1 88.9 %collective-permute-start.5 = (bf16[2,128,768]{1,2,0:T(8,128)(2,1)S(1)}, bf16[2,128,768]{1,2,0:T(8,128)(2,1)S(1)}, u32[]{:S(2)}, u32[]{:S(2)}) collective-permute-start(bf16[2,128,768]{1,2,0:T(8,128)(2,1)S(1)} %pad_maximum_fusion), channel_id=1, source_target_pairs={{0,14},{2,16},{4,18},{6,20},{8,22},{10,24},{12,26},{14,28},{16,30}... | collective-permute-start | bytes 1179656 | tf_op jit(solution)/shard_map/ppermute | solution.py:12
  22.5 96.0 %collective-permute-start.6 = (bf16[2,128,768]{1,2,0:T(8,128)(2,1)S(1)}, bf16[2,128,768]{1,2,0:T(8,128)(2,1)S(1)}, u32[]{:S(2)}, u32[]{:S(2)}) collective-permute-start(bf16[2,128,768]{1,2,0:T(8,128)(2,1)S(1)} %pad_maximum_fusion), channel_id=1, source_target_pairs={{0,10},{2,12},{4,14},{6,16},{8,18},{10,20},{12,22},{14,24},{16,26}... | collective-permute-start | bytes 1179656 | tf_op jit(solution)/shard_map/ppermute | solution.py:12
  24.5 107.2 %collective-permute-start.7 = (bf16[2,128,768]{1,2,0:T(8,128)(2,1)S(1)}, bf16[2,128,768]{1,2,0:T(8,128)(2,1)S(1)}, u32[]{:S(2)}, u32[]{:S(2)}) collective-permute-start(bf16[2,128,768]{1,2,0:T(8,128)(2,1)S(1)} %pad_maximum_fusion), channel_id=1, source_target_pairs={{0,8},{2,10},{4,12},{6,14},{8,16},{10,18},{12,20},{14,22},{16,24},... | collective-permute-start | bytes 1179656 | tf_op jit(solution)/shard_map/ppermute | solution.py:12
  80.6 76.7 %collective-permute-start.8 = (bf16[2,128,768]{1,2,0:T(8,128)(2,1)S(1)}, bf16[2,128,768]{1,2,0:T(8,128)(2,1)S(1)}, u32[]{:S(2)}, u32[]{:S(2)}) collective-permute-start(bf16[2,128,768]{1,2,0:T(8,128)(2,1)S(1)} %pad_maximum_fusion), channel_id=1, source_target_pairs={{0,6},{2,8},{4,10},{6,12},{8,14},{10,16},{12,18},{14,20},{16,22},{... | collective-permute-start | bytes 1179656 | tf_op jit(solution)/shard_map/ppermute | solution.py:12
  94.8 64.6 %collective-permute-start.9 = (bf16[2,128,768]{1,2,0:T(8,128)(2,1)S(1)}, bf16[2,128,768]{1,2,0:T(8,128)(2,1)S(1)}, u32[]{:S(2)}, u32[]{:S(2)}) collective-permute-start(bf16[2,128,768]{1,2,0:T(8,128)(2,1)S(1)} %pad_maximum_fusion), channel_id=1, source_target_pairs={{0,2},{2,4},{4,6},{6,8},{8,10},{10,12},{12,14},{14,16},{16,18},{18... | collective-permute-start | bytes 1179656 | tf_op jit(solution)/shard_map/ppermute | solution.py:12
  110.1 50.8 %collective-permute-start.10 = (bf16[2,128,768]{1,2,0:T(8,128)(2,1)S(1)}, bf16[2,128,768]{1,2,0:T(8,128)(2,1)S(1)}, u32[]{:S(2)}, u32[]{:S(2)}) collective-permute-start(bf16[2,128,768]{1,2,0:T(8,128)(2,1)S(1)} %pad_maximum_fusion), channel_id=1, source_target_pairs={{2,0},{4,2},{6,4},{8,6},{10,8},{12,10},{14,12},{16,14},{18,16},{20... | collective-permute-start | bytes 1179656 | tf_op jit(solution)/shard_map/ppermute | solution.py:12
  118.5 43.7 %collective-permute-start.11 = (bf16[2,128,768]{1,2,0:T(8,128)(2,1)S(1)}, bf16[2,128,768]{1,2,0:T(8,128)(2,1)S(1)}, u32[]{:S(2)}, u32[]{:S(2)}) collective-permute-start(bf16[2,128,768]{1,2,0:T(8,128)(2,1)S(1)} %pad_maximum_fusion), channel_id=1, source_target_pairs={{6,0},{8,2},{10,4},{12,6},{14,8},{16,10},{18,12},{20,14},{22,16},{... | collective-permute-start | bytes 1179656 | tf_op jit(solution)/shard_map/ppermute | solution.py:12
  131.7 31.9 %collective-permute-start.12 = (bf16[2,128,768]{1,2,0:T(8,128)(2,1)S(1)}, bf16[2,128,768]{1,2,0:T(8,128)(2,1)S(1)}, u32[]{:S(2)}, u32[]{:S(2)}) collective-permute-start(bf16[2,128,768]{1,2,0:T(8,128)(2,1)S(1)} %pad_maximum_fusion), channel_id=1, source_target_pairs={{8,0},{10,2},{12,4},{14,6},{16,8},{18,10},{20,12},{22,14},{24,16},... | collective-permute-start | bytes 1179656 | tf_op jit(solution)/shard_map/ppermute | solution.py:12
  157.2 16.9 %collective-permute-start.13 = (bf16[2,128,768]{1,2,0:T(8,128)(2,1)S(1)}, bf16[2,128,768]{1,2,0:T(8,128)(2,1)S(1)}, u32[]{:S(2)}, u32[]{:S(2)}) collective-permute-start(bf16[2,128,768]{1,2,0:T(8,128)(2,1)S(1)} %pad_maximum_fusion), channel_id=1, source_target_pairs={{10,0},{12,2},{14,4},{16,6},{18,8},{20,10},{22,12},{24,14},{26,16}... | collective-permute-start | bytes 1179656 | tf_op jit(solution)/shard_map/ppermute | solution.py:12
  159.4 27.4 %collective-permute-start.14 = (bf16[2,128,768]{1,2,0:T(8,128)(2,1)S(1)}, bf16[2,128,768]{1,2,0:T(8,128)(2,1)S(1)}, u32[]{:S(2)}, u32[]{:S(2)}) collective-permute-start(bf16[2,128,768]{1,2,0:T(8,128)(2,1)S(1)} %pad_maximum_fusion), channel_id=1, source_target_pairs={{14,0},{16,2},{18,4},{20,6},{22,8},{24,10},{26,12},{28,14},{30,16}... | collective-permute-start | bytes 1179656 | tf_op jit(solution)/shard_map/ppermute | solution.py:12
  160.8 33.1 %collective-permute-start.15 = (bf16[2,128,768]{1,2,0:T(8,128)(2,1)S(1)}, bf16[2,128,768]{1,2,0:T(8,128)(2,1)S(1)}, u32[]{:S(2)}, u32[]{:S(2)}) collective-permute-start(bf16[2,128,768]{1,2,0:T(8,128)(2,1)S(1)} %pad_maximum_fusion), channel_id=1, source_target_pairs={{16,0},{18,2},{20,4},{22,6},{24,8},{26,10},{28,12},{30,14},{17,1},... | collective-permute-start | bytes 1179656 | tf_op jit(solution)/shard_map/ppermute | solution.py:12
  162.2 45.2 %collective-permute-start.16 = (bf16[2,128,768]{1,2,0:T(8,128)(2,1)S(1)}, bf16[2,128,768]{1,2,0:T(8,128)(2,1)S(1)}, u32[]{:S(2)}, u32[]{:S(2)}) collective-permute-start(bf16[2,128,768]{1,2,0:T(8,128)(2,1)S(1)} %pad_maximum_fusion), channel_id=1, source_target_pairs={{18,0},{20,2},{22,4},{24,6},{26,8},{28,10},{30,12},{19,1},{21,3},{... | collective-permute-start | bytes 1179656 | tf_op jit(solution)/shard_map/ppermute | solution.py:12
  163.6 43.9 %collective-permute-start.17 = (bf16[2,128,768]{1,2,0:T(8,128)(2,1)S(1)}, bf16[2,128,768]{1,2,0:T(8,128)(2,1)S(1)}, u32[]{:S(2)}, u32[]{:S(2)}) collective-permute-start(bf16[2,128,768]{1,2,0:T(8,128)(2,1)S(1)} %pad_maximum_fusion), channel_id=1, source_target_pairs={{22,0},{24,2},{26,4},{28,6},{30,8},{23,1},{25,3},{27,5},{29,7},{31... | collective-permute-start | bytes 1179656 | tf_op jit(solution)/shard_map/ppermute | solution.py:12
  174.1 33.4 %collective-permute-start.18 = (bf16[2,128,768]{1,2,0:T(8,128)(2,1)S(1)}, bf16[2,128,768]{1,2,0:T(8,128)(2,1)S(1)}, u32[]{:S(2)}, u32[]{:S(2)}) collective-permute-start(bf16[2,128,768]{1,2,0:T(8,128)(2,1)S(1)} %pad_maximum_fusion), channel_id=1, source_target_pairs={{24,0},{26,2},{28,4},{30,6},{25,1},{27,3},{29,5},{31,7}} | collective-permute-start | bytes 1179656 | tf_op jit(solution)/shard_map/ppermute | solution.py:12
  186.8 20.8 %collective-permute-start.19 = (bf16[2,128,768]{1,2,0:T(8,128)(2,1)S(1)}, bf16[2,128,768]{1,2,0:T(8,128)(2,1)S(1)}, u32[]{:S(2)}, u32[]{:S(2)}) collective-permute-start(bf16[2,128,768]{1,2,0:T(8,128)(2,1)S(1)} %pad_maximum_fusion), channel_id=1, source_target_pairs={{26,0},{28,2},{30,4},{27,1},{29,3},{31,5}} | collective-permute-start | bytes 1179656 | tf_op jit(solution)/shard_map/ppermute | solution.py:12
  207.6 4.1 copy-start
Sparse Core Ops, SparseCore 0:
  19.3 152.1 all-gather.1
  478.8 57.9 reduce-scatter.1
where the time goes:
time: 548 us; the launch traced here: 544 us
  waiting for transfers between devices  203 us (37%)
  loops' own time  109 us (20%)
  local copies, waits for them, and re-layouts  107 us (20%)
  starting transfers between devices  50.4 us (9%)
  other arithmetic  39 us (7%)
  matrix products  21.1 us (4%)
  between operations  13.9 us (3%)
    ppermute x20, waiting for transfers between devices, passed_along(): return lax.ppermute(value, axis, pairs)  145 us
    another operation x1, loops' own time, body(): running, _ = lax.scan(visit_band, initial, slot_range)  109 us
    reduce_scatter x1, waiting for transfers between devices, body(): lax.psum_scatter(projection.astype(jnp.bfloat16), 'head', scatter_dimensi...  58.1 us
    ppermute x20, starting transfers between devices, passed_along(): return lax.ppermute(value, axis, pairs)  50.3 us
    reduce_or x27, other arithmetic, visit_band(): is_listed = inside[slot_index] & jnp.any(listed_tiles == key_tile)  35.9 us
    dynamic_slice x27, local copies, waits for them, and re-layouts, visit_band(): key_tile = my_tile + slot_distance[slot_index]  34.7 us
    slice x27, local copies, waits for them, and re-layouts, attend_tile(): value_heads = kv_piece[1].reshape(tok_rows, head_count, head_size)  28.5 us
    dynamic_slice x27, local copies, waits for them, and re-layouts, body(): running, _ = lax.scan(visit_band, initial, slot_range)  17.5 us
  transfers between devices with their start and end apart: 22, of which 11 were waited for; matrix products, arithmetic and copies ran while one was open for 29% of the time, Pallas kernels for 0%

commit v1 on v0

--- a/solution.py
+++ b/solution.py
@@ -1,9 +1,12 @@
 import jax
 import jax.numpy as jnp
 from jax import lax
+from jax.experimental import pallas as pl
+from jax.experimental.pallas import tpu as pltpu
 from jax.sharding import PartitionSpec as P
 
 HD = 128
+MESH = pl.DeviceIdType.MESH
 
 
 def passed_along(value, axis, by):
@@ -30,7 +33,7 @@
     return (new_peak, total_next, summed_next)
 
 
-def body(queries, keys, values, window, out_weight):
+def general_body(queries, keys, values, window, out_weight):
     tok_rows, feat_width = queries.shape
     head_count = feat_width // HD
     tile_count = lax.axis_size("tok")
@@ -93,6 +96,247 @@
     )
 
 
+def column_kernel(
+    q_ref, k_ref, v_ref, win_ref, w_ref, o_ref,
+    qbuf, bias_own, bias, kv, wbuf, wide, m_ref, l_ref, acc_ref, mine, att, part_out, part_in, staged,
+    s_kv, s_q, s_b, s_w, s_fwd, s_sib, s_att, s_part, s_out,
+    r_x, r_y, r_q, r_b, r_w, r_att, r_part, r_out,
+):
+    tile = lax.axis_index("tok")
+    p = lax.axis_index("head")
+    z = tile // 4
+    c = tile % 4
+    z_half = z // 2
+    z_odd = z % 2
+    xn = c + 1 - 2 * (c % 2)
+    dn = 3 - c
+    has_diag = (c == 1) | (c == 2)
+    rows = q_ref.shape[0]
+    span = q_ref.shape[1] // 2
+    heads = span // HD
+    cols = w_ref.shape[1]
+    quarter = 4 * cols
+    scale = HD ** (-0.5)
+
+    def remote(src, dst, ssem, rsem, zt, ct, ht):
+        return pltpu.make_async_remote_copy(
+            src_ref=src, dst_ref=dst, send_sem=ssem, recv_sem=rsem,
+            device_id=(zt * 4 + ct, ht), device_id_type=MESH,
+        )
+
+    sent = []
+
+    def put(src, dst, ssem, rsem, zt, ct, ht):
+        here = (zt == z) & (ht == p)
+
+        @pl.when(here)
+        def _():
+            pltpu.make_async_copy(src, dst, rsem).start()
+
+        @pl.when(jnp.logical_not(here))
+        def _():
+            remote(src, dst, ssem, rsem, zt, ct, ht).start()
+
+        sent.append((jnp.logical_not(here), remote(src, dst, ssem, rsem, zt, ct, ht)))
+
+    def arrived(dst, rsem):
+        pltpu.make_async_copy(dst, dst, rsem).wait()
+
+    barrier = pltpu.get_barrier_semaphore()
+    for k in range(1, 4):
+        for h in range(2):
+            pl.semaphore_signal(barrier, inc=1, device_id=((z + k) % 4 * 4 + c, h), device_id_type=MESH)
+        pl.semaphore_signal(barrier, inc=1, device_id=(z * 4 + (c + k) % 4, p), device_id_type=MESH)
+    pl.semaphore_signal(barrier, inc=1, device_id=(tile, 1 - p), device_id_type=MESH)
+
+    row = lax.broadcasted_iota(jnp.int32, (16, win_ref.shape[1]), 0)
+    slot = row // 4
+    column = jnp.where(slot == 0, c, jnp.where(slot == 1, xn, dn))
+    key_tile = row % 4 * 4 + column
+    listed = jnp.where(win_ref[...] == key_tile, 0.0, -1e30)
+    bias_own[...] = jnp.broadcast_to(jnp.max(listed, axis=1, keepdims=True), bias_own.shape)
+
+    pl.semaphore_wait(barrier, 10)
+
+    for i in range(2):
+        zd = 2 * p + i
+        part = slice(i * span, (i + 1) * span)
+        put(k_ref.at[:, part], kv.at[0, 0, z], s_kv.at[i, 0], r_x.at[0, z], zd, c, 0)
+        put(v_ref.at[:, part], kv.at[1, 0, z], s_kv.at[i, 1], r_x.at[0, z], zd, c, 1)
+    for i in range(2):
+        zd = 2 * p + i
+        part = slice(i * span, (i + 1) * span)
+        put(q_ref.at[:, part], qbuf.at[z_odd], s_q.at[i], r_q.at[z_odd], zd, c, z_half)
+        put(bias_own, bias.at[z_odd], s_b.at[i], r_b.at[z_odd], zd, c, z_half)
+    weight_copies = []
+    for k in range(1, 4):
+        copy = remote(w_ref, wbuf.at[c], s_w.at[k], r_w.at[c], z, (c + k) % 4, p)
+        copy.start()
+        weight_copies.append(copy)
+    own_weight = pltpu.make_async_copy(w_ref, wbuf.at[c], r_w.at[c])
+    own_weight.start()
+
+    plane, diagonal, siblings = [], [], []
+    for k in range(4):
+        zz = (z + k) % 4
+        piece = kv.at[p, 0, zz]
+        arrived(piece, r_x.at[0, zz])
+        copy = remote(piece, kv.at[p, 1, zz], s_fwd.at[0, k], r_x.at[1, zz], z, xn, p)
+        copy.start()
+        plane.append(copy)
+        copy = remote(piece, kv.at[p, 2, zz], s_fwd.at[1, k], r_x.at[2, zz], z, dn, p)
+        pl.when(has_diag)(copy.start)
+        diagonal.append(copy)
+        copy = remote(piece, piece, s_sib.at[0, k], r_y.at[0, zz], z, c, 1 - p)
+        copy.start()
+        siblings.append(copy)
+
+    def share(s):
+        copies = []
+        for k in range(4):
+            zz = (z + k) % 4
+            piece = kv.at[p, s, zz]
+            arrived(piece, r_x.at[s, zz])
+            copy = remote(piece, piece, s_sib.at[s, k], r_y.at[s, zz], z, c, 1 - p)
+            copy.start()
+            copies.append(copy)
+        return copies
+
+    def collect(s):
+        for zz in range(4):
+            arrived(kv.at[1 - p, s, zz], r_y.at[s, zz])
+
+    def attend(s):
+        for j in range(heads):
+            lanes = slice(j * HD, (j + 1) * HD)
+            k_all = kv[0, s, :, :, lanes].reshape(4 * rows, HD)
+            v_all = kv[1, s, :, :, lanes].reshape(4 * rows, HD)
+            for i in range(2):
+                n = j * 2 + i
+                scores = lax.dot_general(
+                    qbuf[i, :, lanes], k_all, (((1,), (1,)), ((), ())), preferred_element_type=jnp.float32
+                )
+                shift = jnp.concatenate([bias[i, s * 4 + t:s * 4 + t + 1, :] for t in range(4)], axis=1)
+                scores = scores * scale + shift
+                top = jnp.max(scores, axis=1, keepdims=True)
+                if s == 0:
+                    peak = top
+                else:
+                    before = m_ref[n][:, :1]
+                    peak = jnp.maximum(before, top)
+                    rescale = jnp.exp(before - peak)
+                unrounded = jnp.exp(scores - peak)
+                total = jnp.sum(unrounded, axis=1, keepdims=True)
+                summed = jnp.dot(unrounded.astype(jnp.bfloat16), v_all, preferred_element_type=jnp.float32)
+                if s > 0:
+                    total = total + l_ref[n][:, :1] * rescale
+                    summed = summed + acc_ref[n] * rescale
+                m_ref[n] = jnp.broadcast_to(peak, (rows, HD))
+                l_ref[n] = jnp.broadcast_to(total, (rows, HD))
+                acc_ref[n] = summed
+
+    for i in range(2):
+        arrived(qbuf.at[i], r_q.at[i])
+        arrived(bias.at[i], r_b.at[i])
+    collect(0)
+    attend(0)
+    siblings += share(1)
+    collect(1)
+    attend(1)
+
+    @pl.when(has_diag)
+    def _():
+        copies = share(2)
+        collect(2)
+        attend(2)
+        for copy in copies:
+            copy.wait_send()
+
+    for j in range(heads):
+        for i in range(2):
+            n = j * 2 + i
+            mine[i * rows:(i + 1) * rows, j * HD:(j + 1) * HD] = (acc_ref[n] / l_ref[n]).astype(jnp.bfloat16)
+
+    for k in range(4):
+        put(mine, att.at[z_odd, p], s_att.at[k], r_att.at[z_odd, p], (z + k) % 4, c, z_half)
+
+    for cc in range(4):
+        arrived(wbuf.at[cc], r_w.at[cc])
+        wide[:, cc * cols:(cc + 1) * cols] = wbuf[cc]
+
+    for zf in range(2):
+        for pp in range(2):
+            arrived(att.at[zf, pp], r_att.at[zf, pp])
+
+    def project(half):
+        return jnp.dot(att[0, half], wide[:span, :], preferred_element_type=jnp.float32) + jnp.dot(
+            att[1, half], wide[span:, :], preferred_element_type=jnp.float32
+        )
+
+    part_out[...] = project(1 - p).astype(jnp.bfloat16)
+    swap = remote(part_out, part_in, s_part, r_part, z, c, 1 - p)
+    swap.start()
+    own = project(p).astype(jnp.bfloat16).astype(jnp.float32)
+    swap.wait_recv()
+    staged[...] = (own + part_in[...].astype(jnp.float32)).astype(jnp.bfloat16)
+
+    place = pl.ds(pl.multiple_of(z_odd * quarter, quarter), quarter)
+    for i in range(2):
+        put(staged.at[i * rows:(i + 1) * rows, :], o_ref.at[:, place], s_out.at[i], r_out.at[z_odd], 2 * p + i, c, z_half)
+    for zf in range(2):
+        arrived(o_ref.at[:, zf * quarter:(zf + 1) * quarter], r_out.at[zf])
+
+    swap.wait_send()
+    for copy in weight_copies + plane + siblings:
+        copy.wait_send()
+
+    @pl.when(has_diag)
+    def _():
+        for copy in diagonal:
+            copy.wait_send()
+
+    for away, copy in sent:
+        pl.when(away)(copy.wait_send)
+
+
+def column_body(queries, keys, values, window, out_weight):
+    rows, width = queries.shape
+    depth, cols = out_weight.shape
+    span = width // 2
+    states = 2 * (span // HD)
+    bf16, f32 = jnp.bfloat16, jnp.float32
+    dma = pltpu.SemaphoreType.DMA
+    vmem = pl.BlockSpec(memory_space=pltpu.VMEM)
+    return pl.pallas_call(
+        column_kernel,
+        out_shape=jax.ShapeDtypeStruct((rows, 8 * cols), bf16),
+        in_specs=[vmem] * 5,
+        out_specs=vmem,
+        scratch_shapes=[
+            pltpu.VMEM((2, rows, span), bf16),
+            pltpu.VMEM((16, 128), f32),
+            pltpu.VMEM((2, 16, 128), f32),
+            pltpu.VMEM((2, 3, 4, rows, span), bf16),
+            pltpu.VMEM((4, depth, cols), bf16),
+            pltpu.VMEM((depth, 4 * cols), bf16),
+            pltpu.VMEM((states, rows, HD), f32),
+            pltpu.VMEM((states, rows, HD), f32),
+            pltpu.VMEM((states, rows, HD), f32),
+            pltpu.VMEM((2 * rows, span), bf16),
+            pltpu.VMEM((2, 2, 2 * rows, span), bf16),
+            pltpu.VMEM((2 * rows, 4 * cols), bf16),
+            pltpu.VMEM((2 * rows, 4 * cols), bf16),
+            pltpu.VMEM((2 * rows, 4 * cols), bf16),
+            dma((2, 2)), dma((2,)), dma((2,)), dma((4,)), dma((2, 4)), dma((3, 4)), dma((4,)), dma, dma((2,)),
+            dma((3, 4)), dma((3, 4)), dma((2,)), dma((2,)), dma((4,)), dma((2, 2)), dma, dma((2,)),
+        ],
+        compiler_params=pltpu.CompilerParams(
+            collective_id=0, has_side_effects=True, vmem_limit_bytes=48 * 1024 * 1024
+        ),
+        cost_estimate=pl.CostEstimate(flops=1300000000, bytes_accessed=3000000, transcendentals=1200000),
+    )(queries, keys, values, window, out_weight)
+
+
 def solution(mesh):
     in_specs = (
         P("tok", "head"),
@@ -102,4 +346,6 @@
         P("head", "tok"),
     )
     out_specs = P("tok", "head")
+    small_grid = mesh.shape["tok"] == 16 and mesh.shape["head"] == 2
+    body = column_body if small_grid else general_body
     return jax.shard_map(body, mesh=mesh, in_specs=in_specs, out_specs=out_specs, check_vma=False)

time: 548 us -> 77.2 us (0.14)
  waiting for transfers between devices: 203 us -> 0 us
  loops' own time: 109 us -> 0 us
  local copies, waits for them, and re-layouts: 107 us -> 1.96 us
  Pallas kernels: 0 us -> 75.1 us
  starting transfers between devices: 50.4 us -> 0 us
  other arithmetic: 39 us -> 0 us
  matrix products: 21.1 us -> 0 us
  between operations: 13.9 us -> 0.06 us
    ppermute x20 -> x0, waiting for transfers between devices: 145 us -> none  [passed_along(): return lax.ppermute(value, axis, pairs)]
    another operation x1 -> x0, loops' own time: 109 us -> none  [body(): running, _ = lax.scan(visit_band, initial, slot_range)]
    pallas_call x0 -> x1, Pallas kernels: none -> 75.1 us  [column_body(): pl.pallas_call(column_kernel, out_shape=jax.ShapeDtypeStruct((rows, 8 * c...]
    dynamic_slice x81 -> x0, local copies, waits for them, and re-layouts: 69.6 us -> none  [the longest x27 34.7 us: visit_band(): key_tile = my_tile + slot_distance[slot_index]]
    reduce_scatter x1 -> x0, waiting for transfers between devices: 58.1 us -> none  [body(): lax.psum_scatter(projection.astype(jnp.bfloat16), 'head', scatter_dimensi...]
    ppermute x20 -> x0, starting transfers between devices: 50.3 us -> none  [passed_along(): return lax.ppermute(value, axis, pairs)]
    reduce_or x27 -> x0, other arithmetic: 35.9 us -> none  [visit_band(): is_listed = inside[slot_index] & jnp.any(listed_tiles == key_tile)]
    slice x27 -> x0, local copies, waits for them, and re-layouts: 28.5 us -> none  [attend_tile(): value_heads = kv_piece[1].reshape(tok_rows, head_count, head_size)]
  transfers between devices with their start and end apart: 22 -> 0, of which waited for: 11 -> 0; matrix products, arithmetic and copies ran while one was open for 29% -> 0% of each run, Pallas kernels for 0% -> 0%
where the time goes in v1:
time: 77.2 us; the launch traced here: 77.1 us
  Pallas kernels  75.1 us (97%)
  local copies, waits for them, and re-layouts  1.96 us (3%)
    pallas_call x1, Pallas kernels, column_body(): pl.pallas_call(column_kernel, out_shape=jax.ShapeDtypeStruct((rows, 8 * c...  75.1 us
    unnamed x10, local copies, waits for them, and re-layouts  1.96 us

profile of v1, /device:TPU:11, one launch (start us, length us, event | category | flops | bytes accessed | tf_op | source)
XLA Modules:
  0.0 77.1 jit_solution(3798506462206881356)
XLA Ops:
  0.0 0.0 copy-start.3
  0.0 0.0 copy-start.2
  0.0 0.0 copy-start.1
  0.0 0.0 copy-start
  0.0 1.2 %copy.6.w_ref = bf16[768,192]{1,0:T(8,128)(2,1)S(1)} copy(bf16[768,192]{0,1:T(8,128)(2,1)} %param.9) | data formatting | bytes 589824 | tf_op args[4]
  1.2 0.0 copy-done.3
  1.2 0.0 copy-done.2
  1.2 0.0 copy-done.1
  1.2 0.0 copy-done
  1.3 75.1 %shard_map.55 = bf16[128,1536]{1,0:T(8,128)(2,1)S(1)} custom-call(bf16[128,768]{1,0:T(8,128)(2,1)S(1)} %copy-done, bf16[128,768]{1,0:T(8,128)(2,1)S(1)} %copy-done.1, bf16[128,768]{1,0:T(8,128)(2,1)S(1)} %copy-done.2, s32[1,27]{1,0:T(1,128)S(1)} %copy-done.3, bf16[768,192]{1,0:T(8,128)(2,1)S(1)} %copy.6.w_ref), custom_call_target="tpu_custom_call" | custom-call | flops 1300000000 | bytes 3000000 | tf_op jit(solution)/shard_map/pallas_call | solution.py:310
  76.3 0.7 copy.8
Async XLA Ops:
  0.0 1.2 %copy-start.3 = (s32[1,27]{1,0:T(1,128)S(1)}, s32[1,27]{1,0:T(1,128)}, u32[]{:S(2)}) copy-start(s32[1,27]{1,0:T(1,128)} %win_ref.1) | copy-start | bytes 328
  0.0 1.2 %copy-start.2 = (bf16[128,768]{1,0:T(8,128)(2,1)S(1)}, bf16[128,768]{1,0:T(8,128)(2,1)}, u32[]{:S(2)}) copy-start(bf16[128,768]{1,0:T(8,128)(2,1)} %v_ref.1) | copy-start | bytes 589828
  0.0 1.2 %copy-start.1 = (bf16[128,768]{1,0:T(8,128)(2,1)S(1)}, bf16[128,768]{1,0:T(8,128)(2,1)}, u32[]{:S(2)}) copy-start(bf16[128,768]{1,0:T(8,128)(2,1)} %k_ref.1) | copy-start | bytes 589828
  0.0 1.2 %copy-start = (bf16[128,768]{1,0:T(8,128)(2,1)S(1)}, bf16[128,768]{1,0:T(8,128)(2,1)}, u32[]{:S(2)}) copy-start(bf16[128,768]{1,0:T(8,128)(2,1)} %q_ref.1) | copy-start | bytes 589828

commit v2 on v0

--- a/solution.py
+++ b/solution.py
@@ -1,9 +1,12 @@
 import jax
 import jax.numpy as jnp
 from jax import lax
+from jax.experimental import pallas as pl
+from jax.experimental.pallas import tpu as pltpu
 from jax.sharding import PartitionSpec as P
 
 HD = 128
+MESH = pl.DeviceIdType.MESH
 
 
 def passed_along(value, axis, by):
@@ -30,7 +33,7 @@
     return (new_peak, total_next, summed_next)
 
 
-def body(queries, keys, values, window, out_weight):
+def general_body(queries, keys, values, window, out_weight):
     tok_rows, feat_width = queries.shape
     head_count = feat_width // HD
     tile_count = lax.axis_size("tok")
@@ -93,6 +96,236 @@
     )
 
 
+def column_kernel(
+    q_ref, k_ref, v_ref, win_ref, w_ref, o_ref,
+    qbuf, bias_own, bias, kv, wide, mine, att, part_out, part_in, staged,
+    send, r_x, r_y, r_q, r_b, r_w, r_att, r_part, r_out,
+):
+    tile = lax.axis_index("tok")
+    p = lax.axis_index("head")
+    z = tile // 4
+    c = tile % 4
+    z_half = z // 2
+    z_odd = z % 2
+    xn = c + 1 - 2 * (c % 2)
+    yn = (c + 2) % 4
+    dn = 3 - c
+    inner = (c == 1) | (c == 2)
+    outer = jnp.logical_not(inner)
+    rows = q_ref.shape[0]
+    span = q_ref.shape[1] // 2
+    heads = span // HD
+    quarter = 4 * w_ref.shape[0]
+    scale = HD ** (-0.5)
+
+    sent = []
+
+    def remote(src, dst, rsem, zt, ct, ht):
+        return pltpu.make_async_remote_copy(
+            src_ref=src, dst_ref=dst, send_sem=send.at[len(sent)], recv_sem=rsem,
+            device_id=(zt * 4 + ct, ht), device_id_type=MESH,
+        )
+
+    def push(src, dst, rsem, zt, ct, ht, when=None):
+        copy = remote(src, dst, rsem, zt, ct, ht)
+        if when is None:
+            copy.start()
+        else:
+            pl.when(when)(copy.start)
+        sent.append((when, copy))
+
+    def put(src, dst, rsem, zt, ct, ht):
+        here = (zt == z) & (ht == p)
+
+        @pl.when(here)
+        def _():
+            pltpu.make_async_copy(src, dst, rsem).start()
+
+        push(src, dst, rsem, zt, ct, ht, jnp.logical_not(here))
+
+    def arrived(dst, rsem):
+        pltpu.make_async_copy(dst, dst, rsem).wait()
+
+    def lanes_of(j, base=0):
+        return slice(base + j * HD, base + (j + 1) * HD)
+
+    barrier = pltpu.get_barrier_semaphore()
+    for k in range(1, 4):
+        for h in range(2):
+            pl.semaphore_signal(barrier, inc=1, device_id=((z + k) % 4 * 4 + c, h), device_id_type=MESH)
+    for ct in (xn, yn):
+        pl.semaphore_signal(barrier, inc=1, device_id=(z * 4 + ct, p), device_id_type=MESH)
+    pl.semaphore_signal(barrier, inc=1, device_id=(tile, 1 - p), device_id_type=MESH)
+
+    row = lax.broadcasted_iota(jnp.int32, (16, win_ref.shape[1]), 0)
+    slot = row // 4
+    column = jnp.where(slot == 0, c, jnp.where(slot == 1, xn, dn))
+    key_tile = row % 4 * 4 + column
+    listed = jnp.where(win_ref[...] == key_tile, 0.0, -1e30)
+    bias_own[...] = jnp.broadcast_to(jnp.max(listed, axis=1, keepdims=True), bias_own.shape)
+
+    pl.semaphore_wait(barrier, 9)
+
+    for j in range(heads):
+        for i in range(2):
+            zd = 2 * p + i
+            here, there = lanes_of(j, i * span), lanes_of(j)
+            put(k_ref.at[:, here], kv.at[0, 0, z, :, there], r_x.at[0, j, z], zd, c, 0)
+            put(v_ref.at[:, here], kv.at[1, 0, z, :, there], r_x.at[0, j, z], zd, c, 1)
+            put(q_ref.at[:, here], qbuf.at[z_odd, :, there], r_q.at[j, z_odd], zd, c, z_half)
+            if j == 0:
+                put(bias_own, bias.at[z_odd], r_b.at[z_odd], zd, c, z_half)
+        if j == 0:
+            for ct in (xn, yn):
+                push(w_ref, wide.at[c], r_w.at[c], z, ct, p)
+            pltpu.make_async_copy(w_ref, wide.at[c], r_w.at[c]).start()
+
+    def spread(j):
+        there = lanes_of(j)
+        for k in range(4):
+            zz = (z + k) % 4
+            piece = kv.at[p, 0, zz, :, there]
+            arrived(piece, r_x.at[0, j, zz])
+            push(piece, kv.at[p, 1, zz, :, there], r_x.at[1, j, zz], z, xn, p)
+            push(piece, piece, r_y.at[0, j, zz], z, c, 1 - p)
+        for k in range(4):
+            zz = (z + k) % 4
+            piece = kv.at[p, 1, zz, :, there]
+            arrived(piece, r_x.at[1, j, zz])
+            push(piece, kv.at[p, 2, zz, :, there], r_x.at[2, j, zz], z, yn, p, outer)
+            push(piece, piece, r_y.at[1, j, zz], z, c, 1 - p)
+        for k in range(4):
+            zz = (z + k) % 4
+            piece = kv.at[p, 2, zz, :, there]
+
+            @pl.when(inner)
+            def _():
+                arrived(piece, r_x.at[2, j, zz])
+
+            push(piece, piece, r_y.at[2, j, zz], z, c, 1 - p, inner)
+
+    def attend_slots(j, slots):
+        there = lanes_of(j)
+        for s in range(slots):
+            for zz in range(4):
+                arrived(kv.at[1 - p, s, zz, :, there], r_y.at[s, j, zz])
+        k_all = kv[0, :slots, :, :, there].reshape(slots * 4 * rows, HD)
+        v_all = kv[1, :slots, :, :, there].reshape(slots * 4 * rows, HD)
+        for i in range(2):
+            scores = lax.dot_general(
+                qbuf[i, :, there], k_all, (((1,), (1,)), ((), ())), preferred_element_type=jnp.float32
+            )
+            shift = jnp.concatenate([bias[i, t:t + 1, :] for t in range(slots * 4)], axis=1)
+            scores = scores * scale + shift
+            peak = jnp.max(scores, axis=1, keepdims=True)
+            unrounded = jnp.exp(scores - peak)
+            total = jnp.sum(unrounded, axis=1, keepdims=True)
+            summed = jnp.dot(unrounded.astype(jnp.bfloat16), v_all, preferred_element_type=jnp.float32)
+            mine[i * rows:(i + 1) * rows, there] = (summed / total).astype(jnp.bfloat16)
+
+    def attend(j):
+        for i in range(2):
+            arrived(qbuf.at[i, :, lanes_of(j)], r_q.at[j, i])
+            if j == 0:
+                arrived(bias.at[i], r_b.at[i])
+        pl.when(inner)(lambda: attend_slots(j, 3))
+        pl.when(outer)(lambda: attend_slots(j, 2))
+        there = lanes_of(j)
+        put(mine.at[:, there], att.at[z_odd, p, :, there], r_att.at[z_odd, p, j], z, c, z_half)
+
+    near = jnp.where(z > 2 * p, 1, 0)
+
+    def carry(j):
+        there = lanes_of(j)
+        for zf in (near, 1 - near):
+            origin = 2 * p + zf
+            for half in range(2):
+                piece = att.at[zf, half, :, there]
+                arrived(piece, r_att.at[zf, half, j])
+                push(piece, piece, r_att.at[zf, half, j], (z + 1) % 4, c, p, (origin <= z) & (z < 3))
+                push(piece, piece, r_att.at[zf, half, j], (z + 3) % 4, c, p, (origin >= z) & (z > 0))
+
+    spread(0)
+    spread(1)
+    for ct in (xn, yn):
+        arrived(wide.at[ct], r_w.at[ct])
+    passed = jnp.where(inner, xn, yn)
+    push(wide.at[passed], wide.at[passed], r_w.at[passed], z, jnp.where(inner, yn, xn), p)
+    attend(0)
+    spread(2)
+    attend(1)
+    carry(0)
+    attend(2)
+    carry(1)
+    carry(2)
+
+    arrived(wide.at[c], r_w.at[c])
+    arrived(wide.at[dn], r_w.at[dn])
+
+    def project(half):
+        sums = [
+            lax.dot_general(
+                att[zf, half], wide[:, :, zf * span:(zf + 1) * span].reshape(quarter, span),
+                (((1,), (1,)), ((), ())), preferred_element_type=jnp.float32,
+            )
+            for zf in range(2)
+        ]
+        return (sums[0] + sums[1]).astype(jnp.bfloat16)
+
+    part_out[...] = project(1 - p)
+    push(part_out, part_in, r_part, z, c, 1 - p)
+    own = project(p).astype(jnp.float32)
+    arrived(part_in, r_part)
+    staged[...] = (own + part_in[...].astype(jnp.float32)).astype(jnp.bfloat16)
+
+    place = pl.ds(pl.multiple_of(z_odd * quarter, quarter), quarter)
+    for i in range(2):
+        put(staged.at[i * rows:(i + 1) * rows, :], o_ref.at[:, place], r_out.at[z_odd], 2 * p + i, c, z_half)
+    for zf in range(2):
+        arrived(o_ref.at[:, zf * quarter:(zf + 1) * quarter], r_out.at[zf])
+
+    for when, copy in sent:
+        if when is None:
+            copy.wait_send()
+        else:
+            pl.when(when)(copy.wait_send)
+
+
+def column_body(queries, keys, values, window, out_weight):
+    rows, width = queries.shape
+    depth, cols = out_weight.shape
+    span = width // 2
+    heads = span // HD
+    bf16, f32 = jnp.bfloat16, jnp.float32
+    dma = pltpu.SemaphoreType.DMA
+    vmem = pl.BlockSpec(memory_space=pltpu.VMEM)
+    copies = heads * (6 + 20 + 1 + 8) + 2 + 3 + 1 + 2
+    return pl.pallas_call(
+        column_kernel,
+        out_shape=jax.ShapeDtypeStruct((rows, 8 * cols), bf16),
+        in_specs=[vmem] * 5,
+        out_specs=vmem,
+        scratch_shapes=[
+            pltpu.VMEM((2, rows, span), bf16),
+            pltpu.VMEM((16, 128), f32),
+            pltpu.VMEM((2, 16, 128), f32),
+            pltpu.VMEM((2, 3, 4, rows, span), bf16),
+            pltpu.VMEM((4, cols, depth), bf16),
+            pltpu.VMEM((2 * rows, span), bf16),
+            pltpu.VMEM((2, 2, 2 * rows, span), bf16),
+            pltpu.VMEM((2 * rows, 4 * cols), bf16),
+            pltpu.VMEM((2 * rows, 4 * cols), bf16),
+            pltpu.VMEM((2 * rows, 4 * cols), bf16),
+            dma((copies,)),
+            dma((3, heads, 4)), dma((3, heads, 4)), dma((heads, 2)), dma((2,)), dma((4,)), dma((2, 2, heads)), dma, dma((2,)),
+        ],
+        compiler_params=pltpu.CompilerParams(
+            collective_id=0, has_side_effects=True, vmem_limit_bytes=48 * 1024 * 1024
+        ),
+        cost_estimate=pl.CostEstimate(flops=1300000000, bytes_accessed=3000000, transcendentals=1200000),
+    )(queries, keys, values, window, out_weight.T)
+
+
 def solution(mesh):
     in_specs = (
         P("tok", "head"),
@@ -102,4 +335,6 @@
         P("head", "tok"),
     )
     out_specs = P("tok", "head")
+    small_grid = mesh.shape["tok"] == 16 and mesh.shape["head"] == 2
+    body = column_body if small_grid else general_body
     return jax.shard_map(body, mesh=mesh, in_specs=in_specs, out_specs=out_specs, check_vma=False)

time: 548 us -> 72.3 us (0.13)
  waiting for transfers between devices: 203 us -> 0 us
  loops' own time: 109 us -> 0 us
  local copies, waits for them, and re-layouts: 107 us -> 5.14 us
  Pallas kernels: 0 us -> 66.9 us
  starting transfers between devices: 50.4 us -> 0 us
  other arithmetic: 39 us -> 0 us
  matrix products: 21.1 us -> 0 us
  between operations: 13.9 us -> 0.01 us
    ppermute x20 -> x0, waiting for transfers between devices: 145 us -> none  [passed_along(): return lax.ppermute(value, axis, pairs)]
    another operation x1 -> x0, loops' own time: 109 us -> none  [body(): running, _ = lax.scan(visit_band, initial, slot_range)]
    dynamic_slice x81 -> x0, local copies, waits for them, and re-layouts: 69.6 us -> none  [the longest x27 34.7 us: visit_band(): key_tile = my_tile + slot_distance[slot_index]]
    pallas_call x0 -> x1, Pallas kernels: none -> 66.9 us  [column_body(): pl.pallas_call(column_kernel, out_shape=jax.ShapeDtypeStruct((rows, 8 * c...]
    reduce_scatter x1 -> x0, waiting for transfers between devices: 58.1 us -> none  [body(): lax.psum_scatter(projection.astype(jnp.bfloat16), 'head', scatter_dimensi...]
    ppermute x20 -> x0, starting transfers between devices: 50.3 us -> none  [passed_along(): return lax.ppermute(value, axis, pairs)]
    reduce_or x27 -> x0, other arithmetic: 35.9 us -> none  [visit_band(): is_listed = inside[slot_index] & jnp.any(listed_tiles == key_tile)]
    slice x27 -> x0, local copies, waits for them, and re-layouts: 28.5 us -> none  [attend_tile(): value_heads = kv_piece[1].reshape(tok_rows, head_count, head_size)]
  transfers between devices with their start and end apart: 22 -> 0, of which waited for: 11 -> 0; matrix products, arithmetic and copies ran while one was open for 29% -> 0% of each run, Pallas kernels for 0% -> 0%
where the time goes in v2:
time: 72.3 us; the launch traced here: 72 us
  Pallas kernels  66.9 us (93%)
  local copies, waits for them, and re-layouts  5.14 us (7%)
    pallas_call x1, Pallas kernels, column_body(): pl.pallas_call(column_kernel, out_shape=jax.ShapeDtypeStruct((rows, 8 * c...  66.9 us
    unnamed x11, local copies, waits for them, and re-layouts  5.14 us

profile of v2, /device:TPU:11, one launch (start us, length us, event | category | flops | bytes accessed | tf_op | source)
XLA Modules:
  0.0 72.0 jit_solution(13470301736857424376)
XLA Ops:
  0.0 0.0 copy-start.4
  0.0 0.7 copy-done.4
  0.7 0.0 copy-start
  0.7 1.0 %copy-done = bf16[768,192]{0,1:T(8,128)(2,1)S(1)} copy-done((bf16[768,192]{0,1:T(8,128)(2,1)S(1)}, bf16[768,192]{0,1:T(8,128)(2,1)}, u32[]{:S(2)}) %copy-start) | copy-done | bytes 294936
  1.6 0.0 copy-start.1
  1.6 0.9 %copy-done.1 = bf16[128,768]{1,0:T(8,128)(2,1)S(1)} copy-done((bf16[128,768]{1,0:T(8,128)(2,1)S(1)}, bf16[128,768]{1,0:T(8,128)(2,1)}, u32[]{:S(2)}) %copy-start.1) | copy-done | bytes 196632
  2.5 0.0 copy-start.2
  2.5 0.9 %copy-done.2 = bf16[128,768]{1,0:T(8,128)(2,1)S(1)} copy-done((bf16[128,768]{1,0:T(8,128)(2,1)S(1)}, bf16[128,768]{1,0:T(8,128)(2,1)}, u32[]{:S(2)}) %copy-start.2) | copy-done | bytes 196632
  3.5 0.0 copy-start.3
  3.5 0.9 %copy-done.3 = bf16[128,768]{1,0:T(8,128)(2,1)S(1)} copy-done((bf16[128,768]{1,0:T(8,128)(2,1)S(1)}, bf16[128,768]{1,0:T(8,128)(2,1)}, u32[]{:S(2)}) %copy-start.3) | copy-done | bytes 196632
  4.4 66.9 %shard_map.55 = bf16[128,1536]{1,0:T(8,128)(2,1)S(1)} custom-call(bf16[128,768]{1,0:T(8,128)(2,1)S(1)} %copy-done.1, bf16[128,768]{1,0:T(8,128)(2,1)S(1)} %copy-done.2, bf16[128,768]{1,0:T(8,128)(2,1)S(1)} %copy-done.3, s32[1,27]{1,0:T(1,128)S(1)} %copy-done.4, bf16[192,768]{1,0:T(8,128)(2,1)S(1)} %bitcast.1), custom_call_target="tpu_custom_call" | custom-call | flops 1300000000 | bytes 3000000 | tf_op jit(solution)/shard_map/pallas_call | solution.py:303
  71.3 0.7 %copy.7 = bf16[128,1536]{1,0:T(8,128)(2,1)} copy(bf16[128,1536]{1,0:T(8,128)(2,1)S(1)} %shard_map.55) | data formatting | bytes 786432
Async XLA Ops:
  0.0 0.7 copy-start.4
  0.7 1.0 %copy-start = (bf16[768,192]{0,1:T(8,128)(2,1)S(1)}, bf16[768,192]{0,1:T(8,128)(2,1)}, u32[]{:S(2)}) copy-start(bf16[768,192]{0,1:T(8,128)(2,1)} %param.9) | copy-start | bytes 884740
  1.6 0.9 %copy-start.1 = (bf16[128,768]{1,0:T(8,128)(2,1)S(1)}, bf16[128,768]{1,0:T(8,128)(2,1)}, u32[]{:S(2)}) copy-start(bf16[128,768]{1,0:T(8,128)(2,1)} %q_ref.1) | copy-start | bytes 589828
  2.5 0.9 %copy-start.2 = (bf16[128,768]{1,0:T(8,128)(2,1)S(1)}, bf16[128,768]{1,0:T(8,128)(2,1)}, u32[]{:S(2)}) copy-start(bf16[128,768]{1,0:T(8,128)(2,1)} %k_ref.1) | copy-start | bytes 589828
  3.5 0.9 %copy-start.3 = (bf16[128,768]{1,0:T(8,128)(2,1)S(1)}, bf16[128,768]{1,0:T(8,128)(2,1)}, u32[]{:S(2)}) copy-start(bf16[128,768]{1,0:T(8,128)(2,1)} %v_ref.1) | copy-start | bytes 589828

commit v3 on v2

--- a/solution.py
+++ b/solution.py
@@ -98,8 +98,8 @@
 
 def column_kernel(
     q_ref, k_ref, v_ref, win_ref, w_ref, o_ref,
-    qbuf, bias_own, bias, kv, wide, mine, att, part_out, part_in, staged,
-    send, r_x, r_y, r_q, r_b, r_w, r_att, r_part, r_out,
+    listing, qbuf, bias_own, bias, kv, wide, mine, att, part_out, part_in, staged,
+    send, s_win, r_x, r_plane, r_y, r_q, r_b, r_w, r_att, r_part, r_out,
 ):
     tile = lax.axis_index("tok")
     p = lax.axis_index("head")
@@ -149,6 +149,8 @@
     def lanes_of(j, base=0):
         return slice(base + j * HD, base + (j + 1) * HD)
 
+    window_copy = pltpu.make_async_copy(win_ref, listing, s_win)
+    window_copy.start()
     barrier = pltpu.get_barrier_semaphore()
     for k in range(1, 4):
         for h in range(2):
@@ -157,11 +159,12 @@
         pl.semaphore_signal(barrier, inc=1, device_id=(z * 4 + ct, p), device_id_type=MESH)
     pl.semaphore_signal(barrier, inc=1, device_id=(tile, 1 - p), device_id_type=MESH)
 
+    window_copy.wait()
     row = lax.broadcasted_iota(jnp.int32, (16, win_ref.shape[1]), 0)
     slot = row // 4
     column = jnp.where(slot == 0, c, jnp.where(slot == 1, xn, dn))
     key_tile = row % 4 * 4 + column
-    listed = jnp.where(win_ref[...] == key_tile, 0.0, -1e30)
+    listed = jnp.where(listing[...] == key_tile, 0.0, -1e30)
     bias_own[...] = jnp.broadcast_to(jnp.max(listed, axis=1, keepdims=True), bias_own.shape)
 
     pl.semaphore_wait(barrier, 9)
@@ -169,10 +172,10 @@
     for j in range(heads):
         for i in range(2):
             zd = 2 * p + i
-            here, there = lanes_of(j, i * span), lanes_of(j)
-            put(k_ref.at[:, here], kv.at[0, 0, z, :, there], r_x.at[0, j, z], zd, c, 0)
-            put(v_ref.at[:, here], kv.at[1, 0, z, :, there], r_x.at[0, j, z], zd, c, 1)
-            put(q_ref.at[:, here], qbuf.at[z_odd, :, there], r_q.at[j, z_odd], zd, c, z_half)
+            here = lanes_of(j, i * span)
+            put(k_ref.at[:, here], kv.at[0, 0, j, z], r_x.at[j, z], zd, c, 0)
+            put(v_ref.at[:, here], kv.at[1, 0, j, z], r_x.at[j, z], zd, c, 1)
+            put(q_ref.at[:, here], qbuf.at[j, z_odd], r_q.at[j, z_odd], zd, c, z_half)
             if j == 0:
                 put(bias_own, bias.at[z_odd], r_b.at[z_odd], zd, c, z_half)
         if j == 0:
@@ -180,40 +183,35 @@
                 push(w_ref, wide.at[c], r_w.at[c], z, ct, p)
             pltpu.make_async_copy(w_ref, wide.at[c], r_w.at[c]).start()
 
-    def spread(j):
-        there = lanes_of(j)
+    def share(s, j, when=None):
+        push(kv.at[p, s, j], kv.at[p, s, j], r_y.at[s, j], z, c, 1 - p, when)
+
+    def spread_own(j):
         for k in range(4):
             zz = (z + k) % 4
-            piece = kv.at[p, 0, zz, :, there]
-            arrived(piece, r_x.at[0, j, zz])
-            push(piece, kv.at[p, 1, zz, :, there], r_x.at[1, j, zz], z, xn, p)
-            push(piece, piece, r_y.at[0, j, zz], z, c, 1 - p)
-        for k in range(4):
-            zz = (z + k) % 4
-            piece = kv.at[p, 1, zz, :, there]
-            arrived(piece, r_x.at[1, j, zz])
-            push(piece, kv.at[p, 2, zz, :, there], r_x.at[2, j, zz], z, yn, p, outer)
-            push(piece, piece, r_y.at[1, j, zz], z, c, 1 - p)
-        for k in range(4):
-            zz = (z + k) % 4
-            piece = kv.at[p, 2, zz, :, there]
-
-            @pl.when(inner)
-            def _():
-                arrived(piece, r_x.at[2, j, zz])
-
-            push(piece, piece, r_y.at[2, j, zz], z, c, 1 - p, inner)
+            piece = kv.at[p, 0, j, zz]
+            arrived(piece, r_x.at[j, zz])
+            push(piece, kv.at[p, 1, j, zz], r_plane.at[0, j], z, xn, p)
+        share(0, j)
+
+    def spread_beside(j):
+        piece = kv.at[p, 1, j]
+        arrived(piece, r_plane.at[0, j])
+        push(piece, kv.at[p, 2, j], r_plane.at[1, j], z, yn, p, outer)
+        share(1, j)
+
+    def spread_diagonal(j):
+        pl.when(inner)(lambda: arrived(kv.at[p, 2, j], r_plane.at[1, j]))
+        share(2, j, inner)
 
     def attend_slots(j, slots):
-        there = lanes_of(j)
         for s in range(slots):
-            for zz in range(4):
-                arrived(kv.at[1 - p, s, zz, :, there], r_y.at[s, j, zz])
-        k_all = kv[0, :slots, :, :, there].reshape(slots * 4 * rows, HD)
-        v_all = kv[1, :slots, :, :, there].reshape(slots * 4 * rows, HD)
+            arrived(kv.at[1 - p, s, j], r_y.at[s, j])
+        k_all = kv[0, :slots, j].reshape(slots * 4 * rows, HD)
+        v_all = kv[1, :slots, j].reshape(slots * 4 * rows, HD)
         for i in range(2):
             scores = lax.dot_general(
-                qbuf[i, :, there], k_all, (((1,), (1,)), ((), ())), preferred_element_type=jnp.float32
+                qbuf[j, i], k_all, (((1,), (1,)), ((), ())), preferred_element_type=jnp.float32
             )
             shift = jnp.concatenate([bias[i, t:t + 1, :] for t in range(slots * 4)], axis=1)
             scores = scores * scale + shift
@@ -221,51 +219,46 @@
             unrounded = jnp.exp(scores - peak)
             total = jnp.sum(unrounded, axis=1, keepdims=True)
             summed = jnp.dot(unrounded.astype(jnp.bfloat16), v_all, preferred_element_type=jnp.float32)
-            mine[i * rows:(i + 1) * rows, there] = (summed / total).astype(jnp.bfloat16)
+            mine[j, i * rows:(i + 1) * rows, :] = (summed / total).astype(jnp.bfloat16)
 
     def attend(j):
         for i in range(2):
-            arrived(qbuf.at[i, :, lanes_of(j)], r_q.at[j, i])
+            arrived(qbuf.at[j, i], r_q.at[j, i])
             if j == 0:
                 arrived(bias.at[i], r_b.at[i])
         pl.when(inner)(lambda: attend_slots(j, 3))
         pl.when(outer)(lambda: attend_slots(j, 2))
-        there = lanes_of(j)
-        put(mine.at[:, there], att.at[z_odd, p, :, there], r_att.at[z_odd, p, j], z, c, z_half)
-
-    near = jnp.where(z > 2 * p, 1, 0)
-
-    def carry(j):
-        there = lanes_of(j)
-        for zf in (near, 1 - near):
-            origin = 2 * p + zf
-            for half in range(2):
-                piece = att.at[zf, half, :, there]
-                arrived(piece, r_att.at[zf, half, j])
-                push(piece, piece, r_att.at[zf, half, j], (z + 1) % 4, c, p, (origin <= z) & (z < 3))
-                push(piece, piece, r_att.at[zf, half, j], (z + 3) % 4, c, p, (origin >= z) & (z > 0))
-
-    spread(0)
-    spread(1)
+        for k in (2, 1, 3, 0):
+            put(mine.at[j], att.at[z_odd, p, j], r_att.at[z_odd, p], (z + k) % 4, c, z_half)
+
+    spread_own(0)
+    spread_own(1)
+    spread_beside(0)
+    spread_own(2)
+    spread_beside(1)
     for ct in (xn, yn):
         arrived(wide.at[ct], r_w.at[ct])
     passed = jnp.where(inner, xn, yn)
     push(wide.at[passed], wide.at[passed], r_w.at[passed], z, jnp.where(inner, yn, xn), p)
+    spread_diagonal(0)
     attend(0)
-    spread(2)
+    spread_beside(2)
+    spread_diagonal(1)
     attend(1)
-    carry(0)
+    spread_diagonal(2)
     attend(2)
-    carry(1)
-    carry(2)
-
+
+    for zf in range(2):
+        for half in range(2):
+            arrived(att.at[zf, half], r_att.at[zf, half])
     arrived(wide.at[c], r_w.at[c])
     arrived(wide.at[dn], r_w.at[dn])
 
     def project(half):
         sums = [
             lax.dot_general(
-                att[zf, half], wide[:, :, zf * span:(zf + 1) * span].reshape(quarter, span),
+                jnp.concatenate([att[zf, half, j] for j in range(heads)], axis=1),
+                wide[:, :, zf * span:(zf + 1) * span].reshape(quarter, span),
                 (((1,), (1,)), ((), ())), preferred_element_type=jnp.float32,
             )
             for zf in range(2)
@@ -299,28 +292,30 @@
     bf16, f32 = jnp.bfloat16, jnp.float32
     dma = pltpu.SemaphoreType.DMA
     vmem = pl.BlockSpec(memory_space=pltpu.VMEM)
-    copies = heads * (6 + 20 + 1 + 8) + 2 + 3 + 1 + 2
+    hbm = pl.BlockSpec(memory_space=pltpu.HBM)
+    copies = heads * (6 + 8 + 4) + 2 + 3 + 1 + 2
     return pl.pallas_call(
         column_kernel,
         out_shape=jax.ShapeDtypeStruct((rows, 8 * cols), bf16),
-        in_specs=[vmem] * 5,
+        in_specs=[hbm] * 5,
         out_specs=vmem,
         scratch_shapes=[
-            pltpu.VMEM((2, rows, span), bf16),
+            pltpu.VMEM((1, window.shape[1]), jnp.int32),
+            pltpu.VMEM((heads, 2, rows, HD), bf16),
             pltpu.VMEM((16, 128), f32),
             pltpu.VMEM((2, 16, 128), f32),
-            pltpu.VMEM((2, 3, 4, rows, span), bf16),
+            pltpu.VMEM((2, 3, heads, 4, rows, HD), bf16),
             pltpu.VMEM((4, cols, depth), bf16),
-            pltpu.VMEM((2 * rows, span), bf16),
-            pltpu.VMEM((2, 2, 2 * rows, span), bf16),
+            pltpu.VMEM((heads, 2 * rows, HD), bf16),
+            pltpu.VMEM((2, 2, heads, 2 * rows, HD), bf16),
             pltpu.VMEM((2 * rows, 4 * cols), bf16),
             pltpu.VMEM((2 * rows, 4 * cols), bf16),
             pltpu.VMEM((2 * rows, 4 * cols), bf16),
-            dma((copies,)),
-            dma((3, heads, 4)), dma((3, heads, 4)), dma((heads, 2)), dma((2,)), dma((4,)), dma((2, 2, heads)), dma, dma((2,)),
+            dma((copies,)), dma,
+            dma((heads, 4)), dma((2, heads)), dma((3, heads)), dma((heads, 2)), dma((2,)), dma((4,)), dma((2, 2)), dma, dma((2,)),
         ],
         compiler_params=pltpu.CompilerParams(
-            collective_id=0, has_side_effects=True, vmem_limit_bytes=48 * 1024 * 1024
+            collective_id=0, has_side_effects=True, vmem_limit_bytes=64 * 1024 * 1024 - 65536
         ),
         cost_estimate=pl.CostEstimate(flops=1300000000, bytes_accessed=3000000, transcendentals=1200000),
     )(queries, keys, values, window, out_weight.T)

time: 72.3 us -> 57.3 us (0.79)
  Pallas kernels: 66.9 us -> 55.3 us
  local copies, waits for them, and re-layouts: 5.14 us -> 1.77 us
    pallas_call x1, Pallas kernels: 66.9 us -> 55.3 us  [column_body(): pl.pallas_call(column_kernel, out_shape=jax.ShapeDtypeStruct((rows, 8 * c...]
    unnamed x11 -> x1, local copies, waits for them, and re-layouts: 5.14 us -> 1.77 us
where the time goes in v3:
time: 57.3 us; the launch traced here: 57.1 us
  Pallas kernels  55.3 us (97%)
  local copies, waits for them, and re-layouts  1.77 us (3%)
    pallas_call x1, Pallas kernels, column_body(): pl.pallas_call(column_kernel, out_shape=jax.ShapeDtypeStruct((rows, 8 * c...  55.3 us
    unnamed x1, local copies, waits for them, and re-layouts  1.77 us

profile of v3, /device:TPU:11, one launch (start us, length us, event | category | flops | bytes accessed | tf_op | source)
XLA Modules:
  0.0 57.1 jit_solution(5526673571259156979)
XLA Ops:
  0.0 55.3 %shard_map.55 = bf16[128,1536]{1,0:T(8,128)(2,1)} custom-call(bf16[128,768]{1,0:T(8,128)(2,1)} %q_ref.1, bf16[128,768]{1,0:T(8,128)(2,1)} %k_ref.1, bf16[128,768]{1,0:T(8,128)(2,1)} %v_ref.1, s32[1,27]{1,0:T(1,128)} %win_ref.1, bf16[192,768]{1,0:T(8,128)(2,1)} %bitcast.1), custom_call_target="tpu_custom_call" | custom-call | flops 1300000000 | bytes 3000000 | tf_op jit(solution)/shard_map/pallas_call | solution.py:297
  55.3 1.8 %copy.7 = bf16[128,1536]{1,0:T(8,128)(2,1)} copy(bf16[128,1536]{1,0:T(8,128)(2,1)} %shard_map.55) | data formatting | bytes 786432

commit v4 on v3

--- a/solution.py
+++ b/solution.py
@@ -98,8 +98,8 @@
 
 def column_kernel(
     q_ref, k_ref, v_ref, win_ref, w_ref, o_ref,
-    listing, qbuf, bias_own, bias, kv, wide, mine, att, part_out, part_in, staged,
-    send, s_win, r_x, r_plane, r_y, r_q, r_b, r_w, r_att, r_part, r_out,
+    listing, qbuf, bias_own, bias, kv, wide, mine, att, part_out, part_in, staged, landed,
+    send, s_win, r_x, r_plane, r_y, r_q, r_b, r_w, r_rev, r_att, r_part, r_out,
 ):
     tile = lax.axis_index("tok")
     p = lax.axis_index("head")
@@ -109,13 +109,16 @@
     z_odd = z % 2
     xn = c + 1 - 2 * (c % 2)
     yn = (c + 2) % 4
+    zn = z + 1 - 2 * z_odd
+    c_odd = c % 2
+    member = z_odd * 2 + c_odd
     dn = 3 - c
     inner = (c == 1) | (c == 2)
     outer = jnp.logical_not(inner)
     rows = q_ref.shape[0]
     span = q_ref.shape[1] // 2
     heads = span // HD
-    quarter = 4 * w_ref.shape[0]
+    cols = w_ref.shape[0]
     scale = HD ** (-0.5)
 
     sent = []
@@ -155,8 +158,8 @@
     for k in range(1, 4):
         for h in range(2):
             pl.semaphore_signal(barrier, inc=1, device_id=((z + k) % 4 * 4 + c, h), device_id_type=MESH)
-    for ct in (xn, yn):
-        pl.semaphore_signal(barrier, inc=1, device_id=(z * 4 + ct, p), device_id_type=MESH)
+    for zt, ct in ((z, xn), (z, yn), (zn, xn)):
+        pl.semaphore_signal(barrier, inc=1, device_id=(zt * 4 + ct, p), device_id_type=MESH)
     pl.semaphore_signal(barrier, inc=1, device_id=(tile, 1 - p), device_id_type=MESH)
 
     window_copy.wait()
@@ -167,7 +170,7 @@
     listed = jnp.where(listing[...] == key_tile, 0.0, -1e30)
     bias_own[...] = jnp.broadcast_to(jnp.max(listed, axis=1, keepdims=True), bias_own.shape)
 
-    pl.semaphore_wait(barrier, 9)
+    pl.semaphore_wait(barrier, 10)
 
     for j in range(heads):
         for i in range(2):
@@ -178,10 +181,6 @@
             put(q_ref.at[:, here], qbuf.at[j, z_odd], r_q.at[j, z_odd], zd, c, z_half)
             if j == 0:
                 put(bias_own, bias.at[z_odd], r_b.at[z_odd], zd, c, z_half)
-        if j == 0:
-            for ct in (xn, yn):
-                push(w_ref, wide.at[c], r_w.at[c], z, ct, p)
-            pltpu.make_async_copy(w_ref, wide.at[c], r_w.at[c]).start()
 
     def share(s, j, when=None):
         push(kv.at[p, s, j], kv.at[p, s, j], r_y.at[s, j], z, c, 1 - p, when)
@@ -219,7 +218,7 @@
             unrounded = jnp.exp(scores - peak)
             total = jnp.sum(unrounded, axis=1, keepdims=True)
             summed = jnp.dot(unrounded.astype(jnp.bfloat16), v_all, preferred_element_type=jnp.float32)
-            mine[j, i * rows:(i + 1) * rows, :] = (summed / total).astype(jnp.bfloat16)
+            mine[j, i] = (summed / total).astype(jnp.bfloat16)
 
     def attend(j):
         for i in range(2):
@@ -228,54 +227,83 @@
                 arrived(bias.at[i], r_b.at[i])
         pl.when(inner)(lambda: attend_slots(j, 3))
         pl.when(outer)(lambda: attend_slots(j, 2))
-        for k in (2, 1, 3, 0):
-            put(mine.at[j], att.at[z_odd, p, j], r_att.at[z_odd, p], (z + k) % 4, c, z_half)
-
+        for i in range(2):
+            put(mine.at[j, i], att.at[i * 2 + c_odd, j, z_odd], r_rev.at[j, z_odd], 2 * p + i, c, z_half)
+
+    def gather(j):
+        for zf in range(2):
+            arrived(att.at[member, j, zf], r_rev.at[j, zf])
+        push(att.at[member, j], att.at[member, j], r_att.at[0, j], zn, c, p)
+        push(att.at[member, j], att.at[member, j], r_att.at[1, j], z, xn, p)
+
+    beside_z = (1 - z_odd) * 2 + c_odd
+    beside_x = z_odd * 2 + 1 - c_odd
+    across = 3 - member
+
+    def relay(j):
+        piece = att.at[beside_z, j]
+        arrived(piece, r_att.at[0, j])
+        push(piece, piece, r_att.at[2, j], z, xn, p)
+
+    b = c // 2
+    own_weight = wide.at[z_half, b]
+    far_weight = wide.at[1 - z_half, b]
+
+    push(w_ref, own_weight, r_w.at[z_half, b], z, yn, p)
+    pltpu.make_async_copy(w_ref, own_weight, r_w.at[z_half, b]).start()
     spread_own(0)
     spread_own(1)
     spread_beside(0)
     spread_own(2)
+    push(w_ref, own_weight, r_w.at[z_half, b], (z + 2) % 4, c, p)
     spread_beside(1)
-    for ct in (xn, yn):
-        arrived(wide.at[ct], r_w.at[ct])
-    passed = jnp.where(inner, xn, yn)
-    push(wide.at[passed], wide.at[passed], r_w.at[passed], z, jnp.where(inner, yn, xn), p)
     spread_diagonal(0)
     attend(0)
     spread_beside(2)
     spread_diagonal(1)
     attend(1)
     spread_diagonal(2)
+    gather(0)
     attend(2)
-
-    for zf in range(2):
-        for half in range(2):
-            arrived(att.at[zf, half], r_att.at[zf, half])
-    arrived(wide.at[c], r_w.at[c])
-    arrived(wide.at[dn], r_w.at[dn])
-
-    def project(half):
-        sums = [
-            lax.dot_general(
-                jnp.concatenate([att[zf, half, j] for j in range(heads)], axis=1),
-                wide[:, :, zf * span:(zf + 1) * span].reshape(quarter, span),
-                (((1,), (1,)), ((), ())), preferred_element_type=jnp.float32,
-            )
-            for zf in range(2)
-        ]
-        return (sums[0] + sums[1]).astype(jnp.bfloat16)
+    gather(1)
+    relay(0)
+    arrived(far_weight, r_w.at[1 - z_half, b])
+    push(far_weight, far_weight, r_w.at[1 - z_half, b], z, yn, p)
+    gather(2)
+    relay(1)
+    relay(2)
+
+    arrived(own_weight, r_w.at[z_half, b])
+    for a in range(2):
+        arrived(wide.at[a, 1 - b], r_w.at[a, 1 - b])
+    for j in range(heads):
+        arrived(att.at[beside_x, j], r_att.at[1, j])
+        arrived(att.at[across, j], r_att.at[2, j])
+
+    def project(a):
+        attended = jnp.concatenate(
+            [att[:, j, zf].reshape(4 * rows, HD) for zf in range(2) for j in range(heads)], axis=1
+        )
+        columns = wide[a].reshape(2 * cols, 2 * span)
+        return lax.dot_general(
+            attended, columns, (((1,), (1,)), ((), ())), preferred_element_type=jnp.float32
+        ).astype(jnp.bfloat16)
 
     part_out[...] = project(1 - p)
     push(part_out, part_in, r_part, z, c, 1 - p)
     own = project(p).astype(jnp.float32)
     arrived(part_in, r_part)
-    staged[...] = (own + part_in[...].astype(jnp.float32)).astype(jnp.bfloat16)
-
-    place = pl.ds(pl.multiple_of(z_odd * quarter, quarter), quarter)
-    for i in range(2):
-        put(staged.at[i * rows:(i + 1) * rows, :], o_ref.at[:, place], r_out.at[z_odd], 2 * p + i, c, z_half)
-    for zf in range(2):
-        arrived(o_ref.at[:, zf * quarter:(zf + 1) * quarter], r_out.at[zf])
+    staged[...] = (own + part_in[...].astype(jnp.float32)).astype(jnp.bfloat16).reshape(staged.shape)
+
+    push(staged.at[across], landed.at[member], r_out.at[member], zn, xn, p)
+    push(staged.at[beside_x], landed.at[member], r_out.at[member], z, xn, p)
+    push(staged.at[beside_z], landed.at[member], r_out.at[member], zn, c, p)
+    landed[member] = staged[member]
+    for m in range(4):
+        pl.when(member != m)(lambda: arrived(landed.at[m], r_out.at[m]))
+        for b_out in range(2):
+            first = (m // 2 * 4 + b_out * 2 + m % 2) * cols
+            o_ref[:, first:first + cols] = landed[m, :, b_out * cols:(b_out + 1) * cols]
 
     for when, copy in sent:
         if when is None:
@@ -293,7 +321,7 @@
     dma = pltpu.SemaphoreType.DMA
     vmem = pl.BlockSpec(memory_space=pltpu.VMEM)
     hbm = pl.BlockSpec(memory_space=pltpu.HBM)
-    copies = heads * (6 + 8 + 4) + 2 + 3 + 1 + 2
+    copies = heads * (6 + 8 + 2 + 3) + 2 + 3 + 1 + 3
     return pl.pallas_call(
         column_kernel,
         out_shape=jax.ShapeDtypeStruct((rows, 8 * cols), bf16),
@@ -305,14 +333,16 @@
             pltpu.VMEM((16, 128), f32),
             pltpu.VMEM((2, 16, 128), f32),
             pltpu.VMEM((2, 3, heads, 4, rows, HD), bf16),
-            pltpu.VMEM((4, cols, depth), bf16),
-            pltpu.VMEM((heads, 2 * rows, HD), bf16),
-            pltpu.VMEM((2, 2, heads, 2 * rows, HD), bf16),
-            pltpu.VMEM((2 * rows, 4 * cols), bf16),
-            pltpu.VMEM((2 * rows, 4 * cols), bf16),
-            pltpu.VMEM((2 * rows, 4 * cols), bf16),
+            pltpu.VMEM((2, 2, cols, depth), bf16),
+            pltpu.VMEM((heads, 2, rows, HD), bf16),
+            pltpu.VMEM((4, heads, 2, rows, HD), bf16),
+            pltpu.VMEM((4 * rows, 2 * cols), bf16),
+            pltpu.VMEM((4 * rows, 2 * cols), bf16),
+            pltpu.VMEM((4, rows, 2 * cols), bf16),
+            pltpu.VMEM((4, rows, 2 * cols), bf16),
             dma((copies,)), dma,
-            dma((heads, 4)), dma((2, heads)), dma((3, heads)), dma((heads, 2)), dma((2,)), dma((4,)), dma((2, 2)), dma, dma((2,)),
+            dma((heads, 4)), dma((2, heads)), dma((3, heads)), dma((heads, 2)), dma((2,)), dma((2, 2)),
+            dma((heads, 2)), dma((3, heads)), dma, dma((4,)),
         ],
         compiler_params=pltpu.CompilerParams(
             collective_id=0, has_side_effects=True, vmem_limit_bytes=64 * 1024 * 1024 - 65536

time: 57.3 us -> 58.8 us (1.026)
  the two profiles are of different devices: /device:TPU:11 before, /device:TPU:0 now
where the time goes in v4:
time: 58.8 us; the launch traced here: 58.6 us
  Pallas kernels  56.8 us (97%)
  local copies, waits for them, and re-layouts  1.77 us (3%)
    pallas_call x1, Pallas kernels, column_body(): pl.pallas_call(column_kernel, out_shape=jax.ShapeDtypeStruct((rows, 8 * c...  56.8 us
    unnamed x1, local copies, waits for them, and re-layouts  1.77 us

profile of v4, /device:TPU:0, one launch (start us, length us, event | category | flops | bytes accessed | tf_op | source)
XLA Modules:
  0.0 58.6 jit_solution(10884608040527837924)
XLA Ops:
  0.0 56.8 %shard_map.55 = bf16[128,1536]{1,0:T(8,128)(2,1)} custom-call(bf16[128,768]{1,0:T(8,128)(2,1)} %q_ref.1, bf16[128,768]{1,0:T(8,128)(2,1)} %k_ref.1, bf16[128,768]{1,0:T(8,128)(2,1)} %v_ref.1, s32[1,27]{1,0:T(1,128)} %win_ref.1, bf16[192,768]{1,0:T(8,128)(2,1)} %bitcast.1), custom_call_target="tpu_custom_call" | custom-call | flops 1300000000 | bytes 3000000 | tf_op jit(solution)/shard_map/pallas_call | solution.py:325
  56.8 1.8 %copy.7 = bf16[128,1536]{1,0:T(8,128)(2,1)} copy(bf16[128,1536]{1,0:T(8,128)(2,1)} %shard_map.55) | data formatting | bytes 786432

commit v5 on v3

--- a/solution.py
+++ b/solution.py
@@ -6,6 +6,7 @@
 from jax.sharding import PartitionSpec as P
 
 HD = 128
+LOG2E = 1.4426950408889634
 MESH = pl.DeviceIdType.MESH
 
 
@@ -98,7 +99,7 @@
 
 def column_kernel(
     q_ref, k_ref, v_ref, win_ref, w_ref, o_ref,
-    listing, qbuf, bias_own, bias, kv, wide, mine, att, part_out, part_in, staged,
+    listing, qbuf, bias_own, bias, kv, wide, mine, att, near_sum, part_out, part_in, staged,
     send, s_win, r_x, r_plane, r_y, r_q, r_b, r_w, r_att, r_part, r_out,
 ):
     tile = lax.axis_index("tok")
@@ -116,7 +117,7 @@
     span = q_ref.shape[1] // 2
     heads = span // HD
     quarter = 4 * w_ref.shape[0]
-    scale = HD ** (-0.5)
+    scale = HD ** (-0.5) * LOG2E
 
     sent = []
 
@@ -169,7 +170,7 @@
 
     pl.semaphore_wait(barrier, 9)
 
-    for j in range(heads):
+    def send_line(j):
         for i in range(2):
             zd = 2 * p + i
             here = lanes_of(j, i * span)
@@ -178,10 +179,6 @@
             put(q_ref.at[:, here], qbuf.at[j, z_odd], r_q.at[j, z_odd], zd, c, z_half)
             if j == 0:
                 put(bias_own, bias.at[z_odd], r_b.at[z_odd], zd, c, z_half)
-        if j == 0:
-            for ct in (xn, yn):
-                push(w_ref, wide.at[c], r_w.at[c], z, ct, p)
-            pltpu.make_async_copy(w_ref, wide.at[c], r_w.at[c]).start()
 
     def share(s, j, when=None):
         push(kv.at[p, s, j], kv.at[p, s, j], r_y.at[s, j], z, c, 1 - p, when)
@@ -209,14 +206,14 @@
             arrived(kv.at[1 - p, s, j], r_y.at[s, j])
         k_all = kv[0, :slots, j].reshape(slots * 4 * rows, HD)
         v_all = kv[1, :slots, j].reshape(slots * 4 * rows, HD)
+        both = lax.dot_general(
+            qbuf[j].reshape(2 * rows, HD), k_all, (((1,), (1,)), ((), ())), preferred_element_type=jnp.float32
+        )
         for i in range(2):
-            scores = lax.dot_general(
-                qbuf[j, i], k_all, (((1,), (1,)), ((), ())), preferred_element_type=jnp.float32
-            )
             shift = jnp.concatenate([bias[i, t:t + 1, :] for t in range(slots * 4)], axis=1)
-            scores = scores * scale + shift
+            scores = both[i * rows:(i + 1) * rows, :] * scale + shift
             peak = jnp.max(scores, axis=1, keepdims=True)
-            unrounded = jnp.exp(scores - peak)
+            unrounded = jnp.exp2(scores - peak)
             total = jnp.sum(unrounded, axis=1, keepdims=True)
             summed = jnp.dot(unrounded.astype(jnp.bfloat16), v_all, preferred_element_type=jnp.float32)
             mine[j, i * rows:(i + 1) * rows, :] = (summed / total).astype(jnp.bfloat16)
@@ -231,39 +228,46 @@
         for k in (2, 1, 3, 0):
             put(mine.at[j], att.at[z_odd, p, j], r_att.at[z_odd, p], (z + k) % 4, c, z_half)
 
+    send_line(0)
+    send_line(1)
     spread_own(0)
+    send_line(2)
     spread_own(1)
+    for ct in (xn, yn):
+        push(w_ref, wide.at[c], r_w.at[c], z, ct, p)
+    pltpu.make_async_copy(w_ref, wide.at[c], r_w.at[c]).start()
     spread_beside(0)
     spread_own(2)
     spread_beside(1)
-    for ct in (xn, yn):
-        arrived(wide.at[ct], r_w.at[ct])
-    passed = jnp.where(inner, xn, yn)
-    push(wide.at[passed], wide.at[passed], r_w.at[passed], z, jnp.where(inner, yn, xn), p)
     spread_diagonal(0)
     attend(0)
     spread_beside(2)
     spread_diagonal(1)
     attend(1)
+    for ct in (xn, yn):
+        arrived(wide.at[ct], r_w.at[ct])
+    passed = jnp.where(inner, xn, yn)
+    push(wide.at[passed], wide.at[passed], r_w.at[passed], z, jnp.where(inner, yn, xn), p)
     spread_diagonal(2)
     attend(2)
-
-    for zf in range(2):
-        for half in range(2):
-            arrived(att.at[zf, half], r_att.at[zf, half])
     arrived(wide.at[c], r_w.at[c])
     arrived(wide.at[dn], r_w.at[dn])
 
+    near = jnp.where(z > 2 * p, 1, 0)
+
+    def features(zf, half):
+        arrived(att.at[zf, half], r_att.at[zf, half])
+        return jnp.concatenate([att[zf, half, j] for j in range(heads)], axis=1)
+
+    def times_weight(attended, zf):
+        columns = wide[:, :, pl.ds(pl.multiple_of(zf * span, span), span)].reshape(quarter, span)
+        return lax.dot_general(attended, columns, (((1,), (1,)), ((), ())), preferred_element_type=jnp.float32)
+
+    for half in range(2):
+        near_sum[half] = times_weight(features(near, half), near)
+
     def project(half):
-        sums = [
-            lax.dot_general(
-                jnp.concatenate([att[zf, half, j] for j in range(heads)], axis=1),
-                wide[:, :, zf * span:(zf + 1) * span].reshape(quarter, span),
-                (((1,), (1,)), ((), ())), preferred_element_type=jnp.float32,
-            )
-            for zf in range(2)
-        ]
-        return (sums[0] + sums[1]).astype(jnp.bfloat16)
+        return (near_sum[half] + times_weight(features(1 - near, half), 1 - near)).astype(jnp.bfloat16)
 
     part_out[...] = project(1 - p)
     push(part_out, part_in, r_part, z, c, 1 - p)
@@ -308,6 +312,7 @@
             pltpu.VMEM((4, cols, depth), bf16),
             pltpu.VMEM((heads, 2 * rows, HD), bf16),
             pltpu.VMEM((2, 2, heads, 2 * rows, HD), bf16),
+            pltpu.VMEM((2, 2 * rows, 4 * cols), f32),
             pltpu.VMEM((2 * rows, 4 * cols), bf16),
             pltpu.VMEM((2 * rows, 4 * cols), bf16),
             pltpu.VMEM((2 * rows, 4 * cols), bf16),

time: 57.3 us -> 62.9 us (1.098)
  Pallas kernels: 55.3 us -> 60.9 us
    pallas_call x1, Pallas kernels: 55.3 us -> 60.9 us  [column_body(): pl.pallas_call(column_kernel, out_shape=jax.ShapeDtypeStruct((rows, 8 * c...]
where the time goes in v5:
time: 62.9 us; the launch traced here: 62.7 us
  Pallas kernels  60.9 us (97%)
  local copies, waits for them, and re-layouts  1.77 us (3%)
    pallas_call x1, Pallas kernels, column_body(): pl.pallas_call(column_kernel, out_shape=jax.ShapeDtypeStruct((rows, 8 * c...  60.9 us
    unnamed x1, local copies, waits for them, and re-layouts  1.77 us

profile of v5, /device:TPU:11, one launch (start us, length us, event | category | flops | bytes accessed | tf_op | source)
XLA Modules:
  0.0 62.7 jit_solution(16822225427633766359)
XLA Ops:
  0.0 60.9 %shard_map.55 = bf16[128,1536]{1,0:T(8,128)(2,1)} custom-call(bf16[128,768]{1,0:T(8,128)(2,1)} %q_ref.1, bf16[128,768]{1,0:T(8,128)(2,1)} %k_ref.1, bf16[128,768]{1,0:T(8,128)(2,1)} %v_ref.1, s32[1,27]{1,0:T(1,128)} %win_ref.1, bf16[192,768]{1,0:T(8,128)(2,1)} %bitcast.1), custom_call_target="tpu_custom_call" | custom-call | flops 1300000000 | bytes 3000000 | tf_op jit(solution)/shard_map/pallas_call | solution.py:301
  60.9 1.8 %copy.7 = bf16[128,1536]{1,0:T(8,128)(2,1)} copy(bf16[128,1536]{1,0:T(8,128)(2,1)} %shard_map.55) | data formatting | bytes 786432

commit v6 on v5

--- a/solution.py
+++ b/solution.py
@@ -206,12 +206,12 @@
             arrived(kv.at[1 - p, s, j], r_y.at[s, j])
         k_all = kv[0, :slots, j].reshape(slots * 4 * rows, HD)
         v_all = kv[1, :slots, j].reshape(slots * 4 * rows, HD)
-        both = lax.dot_general(
-            qbuf[j].reshape(2 * rows, HD), k_all, (((1,), (1,)), ((), ())), preferred_element_type=jnp.float32
-        )
         for i in range(2):
+            scores = lax.dot_general(
+                qbuf[j, i], k_all, (((1,), (1,)), ((), ())), preferred_element_type=jnp.float32
+            )
             shift = jnp.concatenate([bias[i, t:t + 1, :] for t in range(slots * 4)], axis=1)
-            scores = both[i * rows:(i + 1) * rows, :] * scale + shift
+            scores = scores * scale + shift
             peak = jnp.max(scores, axis=1, keepdims=True)
             unrounded = jnp.exp2(scores - peak)
             total = jnp.sum(unrounded, axis=1, keepdims=True)
@@ -228,26 +228,26 @@
         for k in (2, 1, 3, 0):
             put(mine.at[j], att.at[z_odd, p, j], r_att.at[z_odd, p], (z + k) % 4, c, z_half)
 
-    send_line(0)
-    send_line(1)
-    spread_own(0)
-    send_line(2)
-    spread_own(1)
     for ct in (xn, yn):
         push(w_ref, wide.at[c], r_w.at[c], z, ct, p)
     pltpu.make_async_copy(w_ref, wide.at[c], r_w.at[c]).start()
+    send_line(0)
+    send_line(1)
+    send_line(2)
+    spread_own(0)
+    spread_own(1)
     spread_beside(0)
     spread_own(2)
     spread_beside(1)
+    for ct in (xn, yn):
+        arrived(wide.at[ct], r_w.at[ct])
+    passed = jnp.where(inner, xn, yn)
+    push(wide.at[passed], wide.at[passed], r_w.at[passed], z, jnp.where(inner, yn, xn), p)
     spread_diagonal(0)
     attend(0)
     spread_beside(2)
     spread_diagonal(1)
     attend(1)
-    for ct in (xn, yn):
-        arrived(wide.at[ct], r_w.at[ct])
-    passed = jnp.where(inner, xn, yn)
-    push(wide.at[passed], wide.at[passed], r_w.at[passed], z, jnp.where(inner, yn, xn), p)
     spread_diagonal(2)
     attend(2)
     arrived(wide.at[c], r_w.at[c])

time: 62.9 us -> 57.7 us (0.917)
  Pallas kernels: 60.9 us -> 55.8 us
    pallas_call x1, Pallas kernels: 60.9 us -> 55.8 us  [column_body(): pl.pallas_call(column_kernel, out_shape=jax.ShapeDtypeStruct((rows, 8 * c...]
where the time goes in v6:
time: 57.7 us; the launch traced here: 57.6 us
  Pallas kernels  55.8 us (97%)
  local copies, waits for them, and re-layouts  1.77 us (3%)
    pallas_call x1, Pallas kernels, column_body(): pl.pallas_call(column_kernel, out_shape=jax.ShapeDtypeStruct((rows, 8 * c...  55.8 us
    unnamed x1, local copies, waits for them, and re-layouts  1.77 us

profile of v6, /device:TPU:11, one launch (start us, length us, event | category | flops | bytes accessed | tf_op | source)
XLA Modules:
  0.0 57.6 jit_solution(11925377176203935692)
XLA Ops:
  0.0 55.8 %shard_map.55 = bf16[128,1536]{1,0:T(8,128)(2,1)} custom-call(bf16[128,768]{1,0:T(8,128)(2,1)} %q_ref.1, bf16[128,768]{1,0:T(8,128)(2,1)} %k_ref.1, bf16[128,768]{1,0:T(8,128)(2,1)} %v_ref.1, s32[1,27]{1,0:T(1,128)} %win_ref.1, bf16[192,768]{1,0:T(8,128)(2,1)} %bitcast.1), custom_call_target="tpu_custom_call" | custom-call | flops 1300000000 | bytes 3000000 | tf_op jit(solution)/shard_map/pallas_call | solution.py:301
  55.8 1.8 %copy.7 = bf16[128,1536]{1,0:T(8,128)(2,1)} copy(bf16[128,1536]{1,0:T(8,128)(2,1)} %shard_map.55) | data formatting | bytes 786432

commit v7 on v6

--- a/solution.py
+++ b/solution.py
@@ -225,8 +225,19 @@
                 arrived(bias.at[i], r_b.at[i])
         pl.when(inner)(lambda: attend_slots(j, 3))
         pl.when(outer)(lambda: attend_slots(j, 2))
-        for k in (2, 1, 3, 0):
-            put(mine.at[j], att.at[z_odd, p, j], r_att.at[z_odd, p], (z + k) % 4, c, z_half)
+        beyond = jnp.where(z_half == 0, 2, 1)
+        for zt in (beyond, z + 1 - 2 * z_odd, z):
+            put(mine.at[j], att.at[z_odd, p, j], r_att.at[z_odd, p, j], zt, c, z_half)
+
+    hands_on = ((z == 1) & (p == 1)) | ((z == 2) & (p == 0))
+    end = jnp.where(z == 1, 0, 3)
+
+    def hand_on(j):
+        for zf in (p, 1 - p):
+            for half in range(2):
+                piece = att.at[1 - zf, half, j]
+                pl.when(hands_on)(lambda: arrived(piece, r_att.at[1 - zf, half, j]))
+                push(piece, piece, r_att.at[1 - zf, half, j], end, c, p, hands_on)
 
     for ct in (xn, yn):
         push(w_ref, wide.at[c], r_w.at[c], z, ct, p)
@@ -249,14 +260,22 @@
     spread_diagonal(1)
     attend(1)
     spread_diagonal(2)
+    hand_on(0)
     attend(2)
+    hand_on(1)
+    hand_on(2)
     arrived(wide.at[c], r_w.at[c])
     arrived(wide.at[dn], r_w.at[dn])
 
     near = jnp.where(z > 2 * p, 1, 0)
 
     def features(zf, half):
-        arrived(att.at[zf, half], r_att.at[zf, half])
+
+        @pl.when(jnp.logical_not(hands_on))
+        def _():
+            for j in range(heads):
+                arrived(att.at[zf, half, j], r_att.at[zf, half, j])
+
         return jnp.concatenate([att[zf, half, j] for j in range(heads)], axis=1)
 
     def times_weight(attended, zf):
@@ -297,7 +316,7 @@
     dma = pltpu.SemaphoreType.DMA
     vmem = pl.BlockSpec(memory_space=pltpu.VMEM)
     hbm = pl.BlockSpec(memory_space=pltpu.HBM)
-    copies = heads * (6 + 8 + 4) + 2 + 3 + 1 + 2
+    copies = heads * (6 + 8 + 3 + 4) + 2 + 3 + 1 + 2
     return pl.pallas_call(
         column_kernel,
         out_shape=jax.ShapeDtypeStruct((rows, 8 * cols), bf16),
@@ -317,7 +336,7 @@
             pltpu.VMEM((2 * rows, 4 * cols), bf16),
             pltpu.VMEM((2 * rows, 4 * cols), bf16),
             dma((copies,)), dma,
-            dma((heads, 4)), dma((2, heads)), dma((3, heads)), dma((heads, 2)), dma((2,)), dma((4,)), dma((2, 2)), dma, dma((2,)),
+            dma((heads, 4)), dma((2, heads)), dma((3, heads)), dma((heads, 2)), dma((2,)), dma((4,)), dma((2, 2, heads)), dma, dma((2,)),
         ],
         compiler_params=pltpu.CompilerParams(
             collective_id=0, has_side_effects=True, vmem_limit_bytes=64 * 1024 * 1024 - 65536

time: 57.7 us -> 55.9 us (0.969)
  the two profiles are of different devices: /device:TPU:11 before, /device:TPU:9 now
where the time goes in v7:
time: 55.9 us; the launch traced here: 55.7 us
  Pallas kernels  53.9 us (96%)
  local copies, waits for them, and re-layouts  1.77 us (3%)
    pallas_call x1, Pallas kernels, column_body(): pl.pallas_call(column_kernel, out_shape=jax.ShapeDtypeStruct((rows, 8 * c...  53.9 us
    unnamed x1, local copies, waits for them, and re-layouts  1.77 us

profile of v7, /device:TPU:9, one launch (start us, length us, event | category | flops | bytes accessed | tf_op | source)
XLA Modules:
  0.0 55.7 jit_solution(16674330839406336515)
XLA Ops:
  0.0 53.9 %shard_map.55 = bf16[128,1536]{1,0:T(8,128)(2,1)} custom-call(bf16[128,768]{1,0:T(8,128)(2,1)} %q_ref.1, bf16[128,768]{1,0:T(8,128)(2,1)} %k_ref.1, bf16[128,768]{1,0:T(8,128)(2,1)} %v_ref.1, s32[1,27]{1,0:T(1,128)} %win_ref.1, bf16[192,768]{1,0:T(8,128)(2,1)} %bitcast.1), custom_call_target="tpu_custom_call" | custom-call | flops 1300000000 | bytes 3000000 | tf_op jit(solution)/shard_map/pallas_call | solution.py:320
  53.9 1.8 %copy.7 = bf16[128,1536]{1,0:T(8,128)(2,1)} copy(bf16[128,1536]{1,0:T(8,128)(2,1)} %shard_map.55) | data formatting | bytes 786432

commit v8 on v7

--- a/solution.py
+++ b/solution.py
@@ -184,8 +184,7 @@
         push(kv.at[p, s, j], kv.at[p, s, j], r_y.at[s, j], z, c, 1 - p, when)
 
     def spread_own(j):
-        for k in range(4):
-            zz = (z + k) % 4
+        for zz in (z, z + 1 - 2 * z_odd, 2 - z_half, 3 - 3 * z_half):
             piece = kv.at[p, 0, j, zz]
             arrived(piece, r_x.at[j, zz])
             push(piece, kv.at[p, 1, j, zz], r_plane.at[0, j], z, xn, p)
@@ -250,13 +249,13 @@
     spread_beside(0)
     spread_own(2)
     spread_beside(1)
+    spread_diagonal(0)
+    attend(0)
+    spread_beside(2)
     for ct in (xn, yn):
         arrived(wide.at[ct], r_w.at[ct])
     passed = jnp.where(inner, xn, yn)
     push(wide.at[passed], wide.at[passed], r_w.at[passed], z, jnp.where(inner, yn, xn), p)
-    spread_diagonal(0)
-    attend(0)
-    spread_beside(2)
     spread_diagonal(1)
     attend(1)
     spread_diagonal(2)
@@ -292,11 +291,12 @@
     push(part_out, part_in, r_part, z, c, 1 - p)
     own = project(p).astype(jnp.float32)
     arrived(part_in, r_part)
-    staged[...] = (own + part_in[...].astype(jnp.float32)).astype(jnp.bfloat16)
 
     place = pl.ds(pl.multiple_of(z_odd * quarter, quarter), quarter)
     for i in range(2):
-        put(staged.at[i * rows:(i + 1) * rows, :], o_ref.at[:, place], r_out.at[z_odd], 2 * p + i, c, z_half)
+        mid = slice(i * rows, (i + 1) * rows)
+        staged[mid, :] = (own[mid, :] + part_in[mid, :].astype(jnp.float32)).astype(jnp.bfloat16)
+        put(staged.at[mid, :], o_ref.at[:, place], r_out.at[z_odd], 2 * p + i, c, z_half)
     for zf in range(2):
         arrived(o_ref.at[:, zf * quarter:(zf + 1) * quarter], r_out.at[zf])
 
@@ -314,14 +314,13 @@
     heads = span // HD
     bf16, f32 = jnp.bfloat16, jnp.float32
     dma = pltpu.SemaphoreType.DMA
-    vmem = pl.BlockSpec(memory_space=pltpu.VMEM)
     hbm = pl.BlockSpec(memory_space=pltpu.HBM)
     copies = heads * (6 + 8 + 3 + 4) + 2 + 3 + 1 + 2
     return pl.pallas_call(
         column_kernel,
         out_shape=jax.ShapeDtypeStruct((rows, 8 * cols), bf16),
         in_specs=[hbm] * 5,
-        out_specs=vmem,
+        out_specs=hbm,
         scratch_shapes=[
             pltpu.VMEM((1, window.shape[1]), jnp.int32),
             pltpu.VMEM((heads, 2, rows, HD), bf16),

time: 55.9 us -> 54.9 us (0.982)
  the two profiles are of different devices: /device:TPU:9 before, /device:TPU:13 now
where the time goes in v8:
time: 54.9 us; the launch traced here: 54.7 us
  Pallas kernels  52.9 us (96%)
  local copies, waits for them, and re-layouts  1.77 us (3%)
    pallas_call x1, Pallas kernels, column_body(): pl.pallas_call(column_kernel, out_shape=jax.ShapeDtypeStruct((rows, 8 * c...  52.9 us
    unnamed x1, local copies, waits for them, and re-layouts  1.77 us

profile of v8, /device:TPU:13, one launch (start us, length us, event | category | flops | bytes accessed | tf_op | source)
XLA Modules:
  0.0 54.7 jit_solution(1562938817252006372)
XLA Ops:
  0.0 52.9 %shard_map.55 = bf16[128,1536]{1,0:T(8,128)(2,1)} custom-call(bf16[128,768]{1,0:T(8,128)(2,1)} %q_ref.1, bf16[128,768]{1,0:T(8,128)(2,1)} %k_ref.1, bf16[128,768]{1,0:T(8,128)(2,1)} %v_ref.1, s32[1,27]{1,0:T(1,128)} %win_ref.1, bf16[192,768]{1,0:T(8,128)(2,1)} %bitcast.1), custom_call_target="tpu_custom_call" | custom-call | flops 1300000000 | bytes 3000000 | tf_op jit(solution)/shard_map/pallas_call | solution.py:319
  53.0 1.8 %copy.7 = bf16[128,1536]{1,0:T(8,128)(2,1)} copy(bf16[128,1536]{1,0:T(8,128)(2,1)} %shard_map.55) | data formatting | bytes 786432

commit v9 on v8

--- a/solution.py
+++ b/solution.py
@@ -289,22 +289,28 @@
 
     part_out[...] = project(1 - p)
     push(part_out, part_in, r_part, z, c, 1 - p)
-    own = project(p).astype(jnp.float32)
+    own = project(p)
+    near_sum[p] = own.astype(jnp.float32)
     arrived(part_in, r_part)
 
     place = pl.ds(pl.multiple_of(z_odd * quarter, quarter), quarter)
-    for i in range(2):
-        mid = slice(i * rows, (i + 1) * rows)
-        staged[mid, :] = (own[mid, :] + part_in[mid, :].astype(jnp.float32)).astype(jnp.bfloat16)
+    farther = jnp.where(z_half == p, 1 - z_odd, p)
+    for i in (farther, 1 - farther):
+        mid = pl.ds(pl.multiple_of(i * rows, rows), rows)
+        staged[mid, :] = (near_sum[p, mid, :] + part_in[mid, :].astype(jnp.float32)).astype(jnp.bfloat16)
         put(staged.at[mid, :], o_ref.at[:, place], r_out.at[z_odd], 2 * p + i, c, z_half)
+
+    def finish(copies):
+        for when, copy in copies:
+            if when is None:
+                copy.wait_send()
+            else:
+                pl.when(when)(copy.wait_send)
+
+    finish(sent[:-2])
     for zf in range(2):
         arrived(o_ref.at[:, zf * quarter:(zf + 1) * quarter], r_out.at[zf])
-
-    for when, copy in sent:
-        if when is None:
-            copy.wait_send()
-        else:
-            pl.when(when)(copy.wait_send)
+    finish(sent[-2:])
 
 
 def column_body(queries, keys, values, window, out_weight):

time: 54.9 us -> 55.8 us (1.016)
  the two profiles are of different devices: /device:TPU:13 before, /device:TPU:11 now
where the time goes in v9:
time: 55.8 us; the launch traced here: 55.6 us
  Pallas kernels  53.9 us (97%)
  local copies, waits for them, and re-layouts  1.77 us (3%)
    pallas_call x1, Pallas kernels, column_body(): pl.pallas_call(column_kernel, out_shape=jax.ShapeDtypeStruct((rows, 8 * c...  53.9 us
    unnamed x1, local copies, waits for them, and re-layouts  1.77 us

profile of v9, /device:TPU:11, one launch (start us, length us, event | category | flops | bytes accessed | tf_op | source)
XLA Modules:
  0.0 55.6 jit_solution(6091161733723518122)
XLA Ops:
  0.0 53.9 %shard_map.55 = bf16[128,1536]{1,0:T(8,128)(2,1)} custom-call(bf16[128,768]{1,0:T(8,128)(2,1)} %q_ref.1, bf16[128,768]{1,0:T(8,128)(2,1)} %k_ref.1, bf16[128,768]{1,0:T(8,128)(2,1)} %v_ref.1, s32[1,27]{1,0:T(1,128)} %win_ref.1, bf16[192,768]{1,0:T(8,128)(2,1)} %bitcast.1), custom_call_target="tpu_custom_call" | custom-call | flops 1300000000 | bytes 3000000 | tf_op jit(solution)/shard_map/pallas_call | solution.py:325
  53.9 1.8 %copy.7 = bf16[128,1536]{1,0:T(8,128)(2,1)} copy(bf16[128,1536]{1,0:T(8,128)(2,1)} %shard_map.55) | data formatting | bytes 786432

commit v10 on v8

--- a/solution.py
+++ b/solution.py
@@ -243,8 +243,8 @@
     pltpu.make_async_copy(w_ref, wide.at[c], r_w.at[c]).start()
     send_line(0)
     send_line(1)
+    spread_own(0)
     send_line(2)
-    spread_own(0)
     spread_own(1)
     spread_beside(0)
     spread_own(2)

time: 54.9 us -> 54.9 us (level)
  the two profiles are of different devices: /device:TPU:13 before, /device:TPU:11 now
where the time goes in v10:
time: 54.9 us; the launch traced here: 54.6 us
  Pallas kernels  52.8 us (96%)
  local copies, waits for them, and re-layouts  1.77 us (3%)
    pallas_call x1, Pallas kernels, column_body(): pl.pallas_call(column_kernel, out_shape=jax.ShapeDtypeStruct((rows, 8 * c...  52.8 us
    unnamed x1, local copies, waits for them, and re-layouts  1.77 us

profile of v10, /device:TPU:11, one launch (start us, length us, event | category | flops | bytes accessed | tf_op | source)
XLA Modules:
  0.0 54.6 jit_solution(256784888362686369)
XLA Ops:
  0.0 52.8 %shard_map.55 = bf16[128,1536]{1,0:T(8,128)(2,1)} custom-call(bf16[128,768]{1,0:T(8,128)(2,1)} %q_ref.1, bf16[128,768]{1,0:T(8,128)(2,1)} %k_ref.1, bf16[128,768]{1,0:T(8,128)(2,1)} %v_ref.1, s32[1,27]{1,0:T(1,128)} %win_ref.1, bf16[192,768]{1,0:T(8,128)(2,1)} %bitcast.1), custom_call_target="tpu_custom_call" | custom-call | flops 1300000000 | bytes 3000000 | tf_op jit(solution)/shard_map/pallas_call | solution.py:319
  52.8 1.8 %copy.7 = bf16[128,1536]{1,0:T(8,128)(2,1)} copy(bf16[128,1536]{1,0:T(8,128)(2,1)} %shard_map.55) | data formatting | bytes 786432
